TPU v7x, 32 devices: a whole 2x2x4 slice. The times are simulated.
32 devices in a mesh: groups: 2 (over y), lon: 4 (over z), chan: 2 (over x), lat: 2 (over core).
Axes of the slice: x: 2, y: 2, z: 4, core: 2. Of those that a mesh axis runs over, the one named last changes fastest.
Arguments:
- inputs: bfloat16 [256, 64, 512], P('chan', ('groups', 'lat'), 'lon'), parts along dimension 1, may hold values from -6 to 6
- cotangent: bfloat16 [256, 64, 512], P('chan', ('groups', 'lat'), 'lon'), parts along dimension 1, may hold values from -6 to 6
- weight: bfloat16 [3, 3, 256, 256], P(None, None, 'chan'), may hold values from -0.125 to 0.125
- bias_vector: float32 [256], P('chan'), may hold values from -4 to 4
Outputs:
- input_grad: bfloat16 [256, 64, 512], P('chan', ('groups', 'lat'), 'lon'), parts along dimension 1
- weight_grad: float32 [6, 3, 256, 256], P('groups', None, 'chan'), parts along dimension 0
- bias_grad: float32 [512], P(('groups', 'chan')), parts along dimension 0
There are 2 independent parts, one for each index of `groups`. A program takes and returns all parts, laid end to end along the dimension named above; an argument that names none is the same for every part. Nothing has to cross between parts.
All inputs are finite; a program needn't handle non-finite values.
Results may differ from a plain program's by a relative error of at most 0.007.
Values may be sent and summed in bfloat16 or wider, within the bound.
A program may use at most 64 MiB of HBM per device.

v0:
```python
import jax
import jax.numpy as jnp
from jax import lax
from jax.sharding import PartitionSpec as P


def padded_2(shard, sides, width):
    for axis, dim in sides:
        devices, length = (lax.axis_size(axis), shard.shape[dim])
        up = [(i, (i + 1) % devices) for i in range(devices)]
        down = [(j, i) for i, j in up]
        last = lax.slice_in_dim(shard, length - width, length, axis=dim)
        initial = lax.slice_in_dim(shard, 0, width, axis=dim)
        before = lax.ppermute(last, axis, up)
        after = lax.ppermute(initial, axis, down)
        shard = jnp.concatenate([before, shard, after], axis=dim)
    return shard


def gelu_slope(preact):
    normal_cdf = 0.5 * (1.0 + jax.scipy.special.erf(preact * 0.7071067811865476))
    density = jnp.exp(-0.5 * preact * preact) * 0.3989422804014327
    return normal_cdf + preact * density


def mask_rims(padded):
    lat_index = lax.axis_index("lat")
    band_count = lax.axis_size("lat")
    row_ids = jnp.arange(padded.shape[1])
    outside = (row_ids == 0) & (lat_index == 0) | (row_ids == padded.shape[1] - 1) & (
        lat_index == band_count - 1
    )
    return jnp.where(outside[None, :, None], jnp.zeros((), padded.dtype), padded)


def window_of(field, first_row, first_col, row_count, column_count):
    return field[
        :, first_row : first_row + row_count, first_col : first_col + column_count
    ].reshape(field.shape[0], -1)


def local(inputs, cotangent, weight, bias_vector):
    own_channels, row_count, column_count = inputs.shape
    input_pad = mask_rims(padded_2(inputs, (("lon", 2), ("lat", 1)), 1))
    input_all = lax.all_gather(input_pad, "chan", axis=0, tiled=True)
    preact = jnp.zeros((own_channels, row_count * column_count), jnp.float32)
    for tap_row in range(3):
        for tap_col in range(3):
            window = window_of(input_all, tap_row, tap_col, row_count, column_count)
            preact = preact + jnp.dot(
                weight[tap_row, tap_col], window, preferred_element_type=jnp.float32
            )
    preact = preact + bias_vector[:, None]
    upstream = cotangent.reshape(own_channels, -1).astype(jnp.float32)
    grad_pre = (upstream * gelu_slope(preact)).astype(jnp.bfloat16)
    bias_part = jnp.sum(grad_pre.astype(jnp.float32), axis=1)
    taps = []
    for tap_row in range(3):
        row_taps = []
        for tap_col in range(3):
            window = window_of(input_all, tap_row, tap_col, row_count, column_count)
            row_taps.append(
                lax.dot_general(
                    grad_pre, window, (((1,), (1,)), ((), ())), preferred_element_type=jnp.float32
                )
            )
        taps.append(jnp.stack(row_taps))
    weight_part = jnp.stack(taps)
    weight_grad, bias_grad = lax.psum((weight_part, bias_part), ("lon", "lat"))
    grad_field = grad_pre.reshape(own_channels, row_count, column_count)
    grad_pad = mask_rims(padded_2(grad_field, (("lon", 2), ("lat", 1)), 1))
    amount = lax.axis_size("chan") * own_channels
    summed = jnp.zeros((amount, row_count * column_count), jnp.float32)
    for tap_row in range(3):
        for tap_col in range(3):
            kernel_cols = weight[tap_row, tap_col]
            window = window_of(grad_pad, 2 - tap_row, 2 - tap_col, row_count, column_count)
            summed = summed + lax.dot_general(
                kernel_cols, window, (((0,), (0,)), ((), ())), preferred_element_type=jnp.float32
            )
    input_sum = lax.psum_scatter(
        summed.reshape(amount, row_count, column_count), "chan", scatter_dimension=0, tiled=True
    )
    return (input_sum.astype(jnp.bfloat16), weight_grad, bias_grad)


def solution(mesh):
    placed = (
        P("chan", ("groups", "lat"), "lon"),
        P("chan", ("groups", "lat"), "lon"),
        P(None, None, "chan", None),
        P("chan"),
    )
    return jax.shard_map(
        local,
        mesh=mesh,
        in_specs=placed,
        out_specs=(
            P("chan", ("groups", "lat"), "lon"),
            P("groups", None, "chan", None),
            P(("groups", "chan")),
        ),
        check_vma=False,
    )
```

profile of v0, /device:TPU:0, one launch (start us, length us, event | category | flops | bytes accessed | tf_op | source)
XLA Modules:
  0.0 177.4 jit_solution(9235394544272731963)
XLA Ops:
  7.2 1.5 copy.13
  8.8 3.1 %collective-permute-start = (bf16[128,16,1]{0,2,1:T(2,128)(2,1)S(1)}, bf16[128,16,1]{0,2,1:T(2,128)(2,1)S(1)}, u32[]{:S(2)}, u32[]{:S(2)}) collective-permute-start(bf16[128,16,1]{0,2,1:T(2,128)(2,1)S(1)} %get-tuple-element.27), channel_id=1, source_target_pairs={{0,4},{4,8},{8,12},{12,0},{1,5},{5,9},{9,13},{13,1},{2,6},{6,10},{... | collective-permute-start | bytes 12296 | tf_op jit(solution)/shard_map/ppermute | solution.py:14
  11.8 2.1 %collective-permute-start.1 = (bf16[128,16,1]{0,2,1:T(2,128)(2,1)S(1)}, bf16[128,16,1]{0,2,1:T(2,128)(2,1)S(1)}, u32[]{:S(2)}, u32[]{:S(2)}) collective-permute-start(bf16[128,16,1]{0,2,1:T(2,128)(2,1)S(1)} %get-tuple-element.28), channel_id=1, source_target_pairs={{4,0},{8,4},{12,8},{0,12},{5,1},{9,5},{13,9},{1,13},{6,2},{10,6},{... | collective-permute-start | bytes 12296 | tf_op jit(solution)/shard_map/ppermute | solution.py:15
  13.9 1.6 collective-permute-done
  17.0 1.1 maximum_select_fusion
  18.2 1.4 copy.12
  19.6 23.9 %all-gather.2.cloned.1.call-done = bf16[256,18,130]{0,2,1:T(8,128)(2,1)} async-done(((bf16[128,18,130]{0,2,1:T(8,128)(2,1)}), bf16[256,18,130]{0,2,1:T(8,128)(2,1)}) %all-gather.2.cloned.1.call-update) | async-done | bytes 1198096 | tf_op jit(solution)/shard_map/all_gather | solution.py:45
  43.5 8.3 %fusion.46 = (bf16[256,16,128]{0,2,1:T(8,128)(2,1)S(1)}, bf16[256,16,128]{0,2,1:T(8,128)(2,1)S(1)}, bf16[256,16,128]{0,2,1:T(8,128)(2,1)S(1)}, bf16[256,16,128]{...) fusion(bf16[256,18,130]{0,2,1:T(8,128)(2,1)} %all-gather.2.clon, ...), kind=kLoop, calls=%fused_computation.86 | loop fusion | bytes 18874368 | tf_op jit(solution)/shard_map/slice | solution.py:37
  55.6 0.7 copy-done.13
  56.3 0.7 convert_reduce_fusion
  57.1 1.5 collective-permute-start.4
  58.6 2.3 %collective-permute-start.5 = (bf16[128,16,1]{0,2,1:T(2,128)(2,1)S(1)}, bf16[128,16,1]{0,2,1:T(2,128)(2,1)S(1)}, u32[]{:S(2)}, u32[]{:S(2)}) collective-permute-start(bf16[128,16,1]{0,2,1:T(2,128)(2,1)S(1)} %get-tuple-element.26), channel_id=1, source_target_pairs={{4,0},{8,4},{12,8},{0,12},{5,1},{9,5},{13,9},{1,13},{6,2},{10,6},{... | collective-permute-start | bytes 12296 | tf_op jit(solution)/shard_map/ppermute | solution.py:15
  60.9 1.6 collective-permute-done.4
  64.4 0.9 fusion.47
  68.6 1.7 convolution_add_fusion
  70.4 3.0 %copy.16 = f32[256,16,128]{2,1,0:T(8,128)} copy(f32[256,16,128]{0,2,1:T(8,128)} %bitcast.154) | data formatting | bytes 4194304 | tf_op jit(solution)/shard_map/reshape | solution.py:82
  73.6 1.7 convolution_bitcast_fusion
  75.3 1.7 convolution_bitcast_fusion.1
  80.6 1.1 pad_maximum_fusion
  81.8 17.9 %psum.15 = f32[128]{0:T(128)} all-reduce(f32[128]{0:T(128)S(1)} %get-tuple-element.29), channel_id=1, replica_groups=mesh['groups'=2,'lon'=4,'chan'=2,'lat'=2] {'lon','lat'}, use_global_device_ids=true, to_apply=%region_3.4 | all-reduce | flops 128 | bytes 1024 | tf_op jit(solution)/shard_map/psum | solution.py:69
  99.6 6.3 %reduce-scatter.2.cloned.1.call-done = f32[128,16,128]{2,1,0:T(8,128)} async-done(((f32[256,16,128]{2,1,0:T(8,128)}), f32[128,16,128]{2,1,0:T(8,128)}) %reduce-scatter.2.cloned.1.call-update) | async-done | bytes 1048592 | tf_op jit(solution)/shard_map/reduce_scatter | solution.py:81
  105.9 2.1 %convert_element_type.18 = bf16[128,16,128]{2,1,0:T(8,128)(2,1)} convert(f32[128,16,128]{2,1,0:T(8,128)} %reduce-scatter.2.cloned.1.call-done) | non-fusion elementwise | flops 262144 | bytes 1572864 | tf_op jit(solution)/shard_map/convert_element_type | solution.py:84
  108.0 60.5 %all-reduce.2.cloned.1.call-done = f32[3,3,128,256]{3,2,1,0:T(8,128)} async-done(((f32[3,3,128,256]{3,2,1,0:T(8,128)}), f32[3,3,128,256]{3,2,1,0:T(8,128)}) %all-reduce.2.cloned.1.call-update) | async-done | bytes 1179664 | tf_op jit(solution)/shard_map/psum | solution.py:69
  168.5 2.4 %copy.18 = f32[3,3,128,256]{3,2,1,0:T(8,128)} copy(f32[3,3,128,256]{3,2,1,0:T(8,128)} %all-reduce.2.cloned.1.call-done) | data formatting | bytes 2359296
  (78 shorter events, 14.1 us)
Async XLA Ops:
  7.2 11.1 %copy-start.14 = (bf16[128,16,128]{2,1,0:T(8,128)(2,1)S(1)}, bf16[128,16,128]{2,1,0:T(8,128)(2,1)}, u32[]{:S(2)}) copy-start(bf16[128,16,128]{2,1,0:T(8,128)(2,1)} %param.5) | copy-start | bytes 1572868
  7.2 36.3 %all-gather.2.cloned.1.call-start = ((), (), s32[]{:S(2)}) async-start(), calls=%async_computation.1 | async-start | bytes 1880064 | tf_op jit(solution)/shard_map/all_gather | solution.py:45
  8.8 6.8 %collective-permute-start = (bf16[128,16,1]{0,2,1:T(2,128)(2,1)S(1)}, bf16[128,16,1]{0,2,1:T(2,128)(2,1)S(1)}, u32[]{:S(2)}, u32[]{:S(2)}) collective-permute-start(bf16[128,16,1]{0,2,1:T(2,128)(2,1)S(1)} %get-tuple-element.27), channel_id=1, source_target_pairs={{0,4},{4,8},{8,12},{12,0},{1,5},{5,9},{9,13},{13,1},{2,6},{6,10},{... | collective-permute-start | bytes 12296 | tf_op jit(solution)/shard_map/ppermute | solution.py:14
  11.8 3.7 %collective-permute-start.1 = (bf16[128,16,1]{0,2,1:T(2,128)(2,1)S(1)}, bf16[128,16,1]{0,2,1:T(2,128)(2,1)S(1)}, u32[]{:S(2)}, u32[]{:S(2)}) collective-permute-start(bf16[128,16,1]{0,2,1:T(2,128)(2,1)S(1)} %get-tuple-element.28), channel_id=1, source_target_pairs={{4,0},{8,4},{12,8},{0,12},{5,1},{9,5},{13,9},{1,13},{6,2},{10,6},{... | collective-permute-start | bytes 12296 | tf_op jit(solution)/shard_map/ppermute | solution.py:15
  15.6 1.3 collective-permute-start.2
  15.7 1.4 collective-permute-start.3
  18.2 87.8 %reduce-scatter.2.cloned.1.call-start = ((), (), s32[]{:S(2)}) async-start(), calls=%async_computation.2 | async-start | bytes 3145728 | tf_op jit(solution)/shard_map/reduce_scatter | solution.py:81
  19.6 32.3 %copy-start.12 = (bf16[3,3,128,256]{3,2,1,0:T(8,128)(2,1)S(1)}, bf16[3,3,128,256]{3,2,1,0:T(8,128)(2,1)}, u32[]{:S(2)}) copy-start(bf16[3,3,128,256]{3,2,1,0:T(8,128)(2,1)} %param.6) | copy-start | bytes 1769476
  51.9 1.4 copy-start.2
  51.9 1.9 %copy-start.4 = (bf16[256,16,128]{0,2,1:T(8,128)(2,1)}, bf16[256,16,128]{0,2,1:T(8,128)(2,1)S(1)}, u32[]{:S(2)}) copy-start(bf16[256,16,128]{0,2,1:T(8,128)(2,1)S(1)} %get-tuple-element.7) | copy-start | bytes 3145732
  51.9 2.3 %copy-start.6 = (bf16[256,16,128]{0,2,1:T(8,128)(2,1)}, bf16[256,16,128]{0,2,1:T(8,128)(2,1)S(1)}, u32[]{:S(2)}) copy-start(bf16[256,16,128]{0,2,1:T(8,128)(2,1)S(1)} %get-tuple-element.6) | copy-start | bytes 3145732
  51.9 2.7 %copy-start.8 = (bf16[256,16,128]{0,2,1:T(8,128)(2,1)}, bf16[256,16,128]{0,2,1:T(8,128)(2,1)S(1)}, u32[]{:S(2)}) copy-start(bf16[256,16,128]{0,2,1:T(8,128)(2,1)S(1)} %get-tuple-element.5) | copy-start | bytes 3145732
  51.9 3.2 %copy-start.10 = (bf16[256,16,128]{0,2,1:T(8,128)(2,1)}, bf16[256,16,128]{0,2,1:T(8,128)(2,1)S(1)}, u32[]{:S(2)}) copy-start(bf16[256,16,128]{0,2,1:T(8,128)(2,1)S(1)} %get-tuple-element.4) | copy-start | bytes 3145732
  51.9 3.6 %copy-start.11 = (bf16[256,16,128]{0,2,1:T(8,128)(2,1)}, bf16[256,16,128]{0,2,1:T(8,128)(2,1)S(1)}, u32[]{:S(2)}) copy-start(bf16[256,16,128]{0,2,1:T(8,128)(2,1)S(1)} %get-tuple-element.3) | copy-start | bytes 3145732
  55.1 1.2 copy-start.13
  57.1 5.5 %collective-permute-start.4 = (bf16[128,16,1]{0,2,1:T(2,128)(2,1)S(1)}, bf16[128,16,1]{0,2,1:T(2,128)(2,1)S(1)}, u32[]{:S(2)}, u32[]{:S(2)}) collective-permute-start(bf16[128,16,1]{0,2,1:T(2,128)(2,1)S(1)} %get-tuple-element.25), channel_id=1, source_target_pairs={{0,4},{4,8},{8,12},{12,0},{1,5},{5,9},{9,13},{13,1},{2,6},{6,10},{... | collective-permute-start | bytes 12296 | tf_op jit(solution)/shard_map/ppermute | solution.py:14
  58.6 4.0 %collective-permute-start.5 = (bf16[128,16,1]{0,2,1:T(2,128)(2,1)S(1)}, bf16[128,16,1]{0,2,1:T(2,128)(2,1)S(1)}, u32[]{:S(2)}, u32[]{:S(2)}) collective-permute-start(bf16[128,16,1]{0,2,1:T(2,128)(2,1)S(1)} %get-tuple-element.26), channel_id=1, source_target_pairs={{4,0},{8,4},{12,8},{0,12},{5,1},{9,5},{13,9},{1,13},{6,2},{10,6},{... | collective-permute-start | bytes 12296 | tf_op jit(solution)/shard_map/ppermute | solution.py:15
  62.6 1.3 collective-permute-start.6
  62.7 1.4 collective-permute-start.7
  73.4 95.1 %all-reduce.2.cloned.1.call-start = ((), (), s32[]{:S(2)}) async-start(), calls=%async_computation.3 | async-start | bytes 2359296 | tf_op jit(solution)/shard_map/psum | solution.py:69
  73.6 3.3 %copy-start.9 = (bf16[256,16,128]{0,2,1:T(8,128)(2,1)S(1)}, bf16[256,16,128]{0,2,1:T(8,128)(2,1)}, u32[]{:S(2)}) copy-start(bf16[256,16,128]{0,2,1:T(8,128)(2,1)} %copy-done.8) | copy-start | bytes 3145732
  75.3 2.1 %copy-start.7 = (bf16[256,16,128]{0,2,1:T(8,128)(2,1)S(1)}, bf16[256,16,128]{0,2,1:T(8,128)(2,1)}, u32[]{:S(2)}) copy-start(bf16[256,16,128]{0,2,1:T(8,128)(2,1)} %copy-done.6) | copy-start | bytes 3145732
  77.4 1.3 copy-start.3
  78.2 1.3 copy-start.1
  (3 other events, 3.5 us)
Sparse Core Ops, SparseCore 0:
  18.3 25.1 all-gather.1
  73.5 32.3 reduce-scatter.1
  109.0 59.5 all-reduce.1
where the time goes:
time: 178 us; the launch traced here: 177 us
  waiting for transfers between devices  95.8 us (54%)
  local copies, waits for them, and re-layouts  19.5 us (11%)
  blocking collectives  17.9 us (10%)
  matrix products  15 us (8%)
  between operations  14.2 us (8%)
  starting transfers between devices  10.5 us (6%)
  other arithmetic  4.73 us (3%)
    psum x1, waiting for transfers between devices, local(): weight_grad, bias_grad = lax.psum((weight_part, bias_part), ('lon', 'lat'))  60.5 us
    all_gather x1, waiting for transfers between devices, local(): input_all = lax.all_gather(input_pad, 'chan', axis=0, tiled=True)  23.9 us
    psum x1, blocking collectives, local(): weight_grad, bias_grad = lax.psum((weight_part, bias_part), ('lon', 'lat'))  17.9 us
    slice x2, local copies, waits for them, and re-layouts, window_of(): field[:, first_row:first_row + row_count, first_col:first_col + column_co...  9.24 us
    reduce_scatter x1, waiting for transfers between devices, local(): lax.psum_scatter(summed.reshape(amount, row_count, column_count), 'chan',...  6.31 us
    unnamed x34, local copies, waits for them, and re-layouts  5.76 us
    dot_general x9, matrix products, local(): lax.dot_general(grad_pre, window, (((1,), (1,)), ((), ())), preferred_ele...  5.76 us
    ppermute x4, starting transfers between devices, padded_2(): after = lax.ppermute(initial, axis, down)  5.42 us
  transfers between devices with their start and end apart: 11, of which 9 were waited for; matrix products, arithmetic and copies ran while one was open for 6% of the time, Pallas kernels for 0%

commit v1 on v0

v1 whole, which is shorter than its diff:
```python
import functools

import jax
import jax.numpy as jnp
from jax import lax
from jax.experimental import pallas as pl
from jax.experimental.pallas import tpu as pltpu
from jax.sharding import PartitionSpec as P

MESH = pl.DeviceIdType.MESH
BF = jnp.bfloat16
F32 = jnp.float32
PIECES = 4


def gelu_slope(preact):
    normal_cdf = 0.5 * (1.0 + lax.erf(preact * 0.7071067811865476))
    density = jnp.exp(-0.5 * preact * preact) * 0.3989422804014327
    return normal_cdf + preact * density


def nt(a, b):
    return lax.dot_general(a, b, (((1,), (1,)), ((), ())), preferred_element_type=F32)


def kernel(
    sizes,
    x_ref, ct_ref, w_ref, b_ref,
    dx_ref, dw_ref, db_ref,
    xs, hx, hc, edge, shift, w2, wt, gs, hg, hgc, gedge,
    dwp, dwsend, dwcore, zsend, zrecv, gathered, bias, dxf, dxs, dxr,
    x_sem, row_sem, col_sem, grow_sem, gcol_sem, core_sem, rs_sem, ag_sem, fwd_sem, bias_sem, dx_sem,
):
    nlon, nchan, nlat, C, CA, H, W, R = sizes
    L = H * W
    part = L // PIECES
    group = lax.axis_index("groups")
    lon = lax.axis_index("lon")
    chan = lax.axis_index("chan")
    lat = lax.axis_index("lat")
    other = 1 - lat

    def at(a, b, c):
        return (group, a, b, c)

    def copy(src, dst, sems, index, device):
        return pltpu.make_async_remote_copy(
            src_ref=src, dst_ref=dst,
            send_sem=sems.at[(0,) + index], recv_sem=sems.at[(1,) + index],
            device_id=device, device_id_type=MESH,
        )

    everyone = nlon * nchan * nlat
    me = (lon * nchan + chan) * nlat + lat
    barrier = pltpu.get_barrier_semaphore()

    @pl.loop(1, everyone)
    def _(d):
        peer = lax.rem(me + d, everyone)
        pl.semaphore_signal(
            barrier, inc=1, device_id_type=MESH,
            device_id=at(peer // (nchan * nlat), lax.rem(peer // nlat, nchan), lax.rem(peer, nlat)),
        )

    def edges(field):
        row = lax.broadcasted_iota(jnp.int32, (2 * H, L), 0)
        lane = lax.broadcasted_iota(jnp.int32, (2 * H, L), 1)
        want = jnp.where(row < H, row * W, (row - H) * W + W - 1)
        pick = jnp.where(lane == want, 1.0, 0.0).astype(BF)
        return nt(pick, field).astype(BF)

    edge[...] = edges(x_ref[...])
    mine = pl.ds(pl.multiple_of(chan * C, C), C)
    xs[1, mine, pl.ds(W, L)] = x_ref[...]
    rim = pl.ds(pl.multiple_of(lat * (H + 1) * W, W), W)
    xs[1, :, rim] = jnp.zeros((CA, W), BF)
    gs[1, :, rim] = jnp.zeros((C, W), BF)
    pl.semaphore_wait(barrier, everyone - 1)

    from_row = pl.ds(pl.multiple_of(other * (H - 1) * W, W), W)
    to_row = pl.ds(pl.multiple_of(lat * 0 + (1 - other) * 0 + other * 0 + lat * (H + 1) * W, W), W)
    x_copies, halo_copies = [], []
    for d in range(nchan):
        there = lax.rem(chan + d, nchan)
        halo_copies.append(
            copy(x_ref.at[:, from_row], xs.at[1, mine, to_row], row_sem, (d,), at(lon, there, other))
        )
        for side in range(2):
            lon_to = lax.rem(lon + (nlon - 1 if side == 0 else 1), nlon)
            for dl in range(2):
                halo_copies.append(
                    copy(
                        edge.at[pl.ds(side * H, H)],
                        hx.at[chan, pl.ds(((1 - side) * 2 + dl) * H, H)],
                        col_sem, (d, side, dl),
                        at(lon_to, there, lat if dl == 0 else other),
                    )
                )
    for c in halo_copies:
        c.start()
    for piece in range(PIECES):
        for d in range(1, nchan):
            c = copy(
                x_ref.at[:, pl.ds(piece * part, part)],
                xs.at[1, mine, pl.ds(W + piece * part, part)],
                x_sem, (d, piece), at(lon, lax.rem(chan + d, nchan), lat),
            )
            c.start()
            x_copies.append(c)

    @pl.loop(0, H + 2)
    def _(r):
        k = lax.broadcasted_iota(jnp.int32, (W + 128, 2 * W), 0)
        n = lax.broadcasted_iota(jnp.int32, (W + 128, 2 * W), 1)
        first = jnp.where(lat == 1, 2 * H - 1, -1000)
        last = jnp.where(lat == 0, H, -1000)
        held = jnp.where(r == 0, first, jnp.where(r == H + 1, last, r - 1))
        right = n >= W
        col = jnp.where(right, n - W, n)
        want = jnp.where(right, col + 1, col - 1)
        want = jnp.where(right & (col == W - 1), W + 2 * H + held, want)
        want = jnp.where((~right) & (col == 0), W + held, want)
        hit = jnp.where(k == want, 1.0, 0.0).astype(BF)
        shift[:, pl.ds(pl.multiple_of(r * 2 * W, 2 * W), 2 * W)] = hit

    for t in range(9):
        w2[:, pl.ds(t * CA, CA)] = w_ref[pl.ds(t * C, C), :]
    wt[...] = jnp.transpose(w_ref[...].astype(F32)).astype(BF)

    def build_shifts(field, columns):
        @pl.loop(0, H + 2)
        def _(r):
            here = pl.ds(pl.multiple_of(r * W, W), W)
            both = jnp.concatenate([field[1, :, here], columns[...]], axis=1)
            moved = jnp.dot(
                both, shift[:, pl.ds(pl.multiple_of(r * 2 * W, 2 * W), 2 * W)],
                preferred_element_type=F32,
            ).astype(BF)
            field[0, :, here] = moved[:, :W]
            field[2, :, here] = moved[:, W:]

    def turned(block):
        full = jnp.concatenate([block, jnp.zeros((128 - block.shape[0], block.shape[1]), BF)], axis=0)
        return jnp.transpose(full.astype(F32)).astype(BF)

    for c in halo_copies:
        c.wait()
    for k in range(nchan):
        hc[pl.ds(k * C, C), :] = turned(hx[k])
    for c in x_copies:
        c.wait()
    build_shifts(xs, hc)

    @pl.loop(0, PIECES)
    def _(piece):
        def lanes(p):
            return pl.ds(pl.multiple_of(p * W + piece * part, W), part)

        stack = jnp.concatenate(
            [xs[q, :, lanes(p)] for p in range(3) for q in range(3)], axis=0
        )
        preact = jnp.dot(w2[...], stack, preferred_element_type=F32) + b_ref[...]
        upstream = ct_ref[:, lanes(0)].astype(F32)
        gs[1, :, lanes(1)] = (upstream * gelu_slope(preact)).astype(BF)

    gedge[...] = edges(gs[1, :, pl.ds(W, L)])
    grad_from = pl.ds(pl.multiple_of(W + other * (H - 1) * W, W), W)
    grad_copies = [copy(gs.at[1, :, grad_from], gs.at[1, :, to_row], grow_sem, (0,), at(lon, chan, other))]
    for side in range(2):
        lon_to = lax.rem(lon + (nlon - 1 if side == 0 else 1), nlon)
        for dl in range(2):
            grad_copies.append(
                copy(
                    gedge.at[pl.ds(side * H, H)],
                    hg.at[pl.ds(((1 - side) * 2 + dl) * H, H)],
                    gcol_sem, (side, dl), at(lon_to, chan, lat if dl == 0 else other),
                )
            )
    for c in grad_copies:
        c.start()

    ring = nlon * nlat
    spot = lon * nlat + lat
    bias[spot] = nt(jnp.ones((8, L), BF), gs[1, :, pl.ds(W, L)])
    bias_copies = []
    for d in range(1, ring):
        peer = lax.rem(spot + d, ring)
        c = copy(bias.at[spot], bias.at[spot], bias_sem, (d,), at(peer // nlat, chan, lax.rem(peer, nlat)))
        c.start()
        bias_copies.append(c)

    if R > 9 * C:
        dwp[pl.ds(9 * C, R - 9 * C), :] = jnp.zeros((R - 9 * C, CA), F32)
    for p in range(3):
        for q in range(3):
            dwp[pl.ds((p * 3 + q) * C, C), :] = nt(
                gs[1, :, pl.ds(W, L)], xs[q, :, pl.ds(p * W, L)]
            )
    half = R // 2
    quarter = half // nlon
    dwsend[...] = dwp[pl.ds(pl.multiple_of(other * half, half), half), :].astype(BF)
    core_copy = copy(dwsend, dwcore, core_sem, (0,), at(lon, chan, other))
    core_copy.start()

    for c in grad_copies:
        c.wait()
    hgc[...] = turned(hg[...])
    build_shifts(gs, hgc)

    @pl.loop(0, PIECES)
    def _(piece):
        def lanes(p):
            return pl.ds(pl.multiple_of(p * W + piece * part, W), part)

        stack = jnp.concatenate(
            [gs[2 - q, :, lanes(2 - p)] for p in range(3) for q in range(3)], axis=0
        )
        whole = jnp.dot(wt[...], stack, preferred_element_type=F32)
        dxf[:, lanes(0)] = whole
        dxs[:, lanes(0)] = whole.astype(BF)
        for d in range(1, nchan):
            there = lax.rem(chan + d, nchan)
            theirs = pl.ds(pl.multiple_of(there * C, C), C)
            copy(
                dxs.at[theirs, lanes(0)], dxr.at[d, :, lanes(0)], dx_sem, (d, piece), at(lon, there, lat)
            ).start()

    core_copy.wait()
    base = lat * half
    own_half = pl.ds(pl.multiple_of(base, half), half)
    summed = dwp[own_half, :] + dwcore[...].astype(F32)
    dwp[own_half, :] = summed
    zsend[...] = summed.astype(BF)
    rs_copies = []
    for d in range(1, nlon):
        there = lax.rem(lon + d, nlon)
        c = copy(
            zsend.at[pl.ds(pl.multiple_of(there * quarter, 16), quarter), :],
            zrecv.at[d], rs_sem, (d,), at(there, chan, lat),
        )
        c.start()
        rs_copies.append(c)
    for c in rs_copies:
        c.wait()
    own_rows = pl.ds(pl.multiple_of(base + lon * quarter, 16), quarter)
    total = dwp[own_rows, :]
    for d in range(1, nlon):
        total = total + zrecv[d].astype(F32)
    gathered[own_rows, :] = total.astype(BF)
    ag_copies, fwd_copies = [], []
    for d in range(1, nlon):
        c = copy(
            gathered.at[own_rows, :], gathered.at[own_rows, :], ag_sem, (d,),
            at(lax.rem(lon + d, nlon), chan, lat),
        )
        c.start()
        ag_copies.append(c)
    for d in range(nlon):
        if d > 0:
            ag_copies[d - 1].wait_recv()
        source = lax.rem(lon + nlon - d, nlon)
        rows = pl.ds(pl.multiple_of(base + source * quarter, 16), quarter)
        c = copy(gathered.at[rows, :], gathered.at[rows, :], fwd_sem, (d,), at(lon, chan, other))
        c.start()
        fwd_copies.append(c)

    for piece in range(PIECES):
        here = pl.ds(piece * part, part)
        acc = dxf[mine, here]
        for d in range(1, nchan):
            there = lax.rem(chan + d, nchan)
            theirs = pl.ds(pl.multiple_of(there * C, C), C)
            copy(dxs.at[theirs, here], dxr.at[d, :, here], dx_sem, (d, piece), at(lon, there, lat)).wait()
            acc = acc + dxr[d, :, here].astype(F32)
        dx_ref[:, here] = acc.astype(BF)

    for c in bias_copies:
        c.wait()
    db_ref[...] = jnp.sum(bias[...], axis=0)
    for c in ag_copies:
        c.wait_send()
    for c in fwd_copies:
        c.wait()
    dw_ref[...] = gathered[...]


def local(nlon, nchan, nlat, inputs, cotangent, weight, bias_vector):
    C, H, W = inputs.shape
    CA = weight.shape[3]
    L = H * W
    step = nlat * nlon * 16
    R = -(-9 * C // step) * step
    half = R // nlat
    sizes = (nlon, nchan, nlat, C, CA, H, W, R)
    wide = (H + 2) * W
    vmem = pl.BlockSpec(memory_space=pltpu.VMEM)
    dma = pltpu.SemaphoreType.DMA
    dx, dw, db = pl.pallas_call(
        functools.partial(kernel, sizes),
        out_shape=(
            jax.ShapeDtypeStruct((C, L), BF),
            jax.ShapeDtypeStruct((R, CA), BF),
            jax.ShapeDtypeStruct((8, C), F32),
        ),
        in_specs=[vmem] * 4,
        out_specs=(vmem,) * 3,
        scratch_shapes=[
            pltpu.VMEM((3, CA, wide), BF),
            pltpu.VMEM((nchan, 4 * H, C), BF),
            pltpu.VMEM((CA, 128), BF),
            pltpu.VMEM((2 * H, C), BF),
            pltpu.VMEM((W + 128, (H + 2) * 2 * W), BF),
            pltpu.VMEM((C, 9 * CA), BF),
            pltpu.VMEM((CA, 9 * C), BF),
            pltpu.VMEM((3, C, wide), BF),
            pltpu.VMEM((4 * H, C), BF),
            pltpu.VMEM((C, 128), BF),
            pltpu.VMEM((2 * H, C), BF),
            pltpu.VMEM((R, CA), F32),
            pltpu.VMEM((half, CA), BF),
            pltpu.VMEM((half, CA), BF),
            pltpu.VMEM((half, CA), BF),
            pltpu.VMEM((nlon, half // nlon, CA), BF),
            pltpu.VMEM((R, CA), BF),
            pltpu.VMEM((nlon * nlat, 8, C), F32),
            pltpu.VMEM((CA, L), F32),
            pltpu.VMEM((CA, L), BF),
            pltpu.VMEM((nchan, C, L), BF),
            dma((2, nchan, PIECES)),
            dma((2, nchan)),
            dma((2, nchan, 2, 2)),
            dma((2, 1)),
            dma((2, 2, 2)),
            dma((2, 1)),
            dma((2, nlon)),
            dma((2, nlon)),
            dma((2, nlon)),
            dma((2, nlon * nlat)),
            dma((2, nchan, PIECES)),
        ],
        compiler_params=pltpu.CompilerParams(
            collective_id=0, has_side_effects=True, vmem_limit_bytes=48 * 1024 * 1024
        ),
        cost_estimate=pl.CostEstimate(
            flops=3 * 2 * 9 * C * CA * L, bytes_accessed=4 * C * L * 2, transcendentals=2 * C * L
        ),
        name="conv_backward",
    )(
        inputs.reshape(C, L),
        cotangent.reshape(C, L),
        weight.reshape(9 * C, CA),
        bias_vector.reshape(C, 1),
    )
    weight_grad = dw[: 9 * C].astype(F32).reshape(3, 3, C, CA)
    return dx.reshape(C, H, W), weight_grad, db[0]


def solution(mesh):
    shape = mesh.shape
    placed = (
        P("chan", ("groups", "lat"), "lon"),
        P("chan", ("groups", "lat"), "lon"),
        P(None, None, "chan", None),
        P("chan"),
    )
    return jax.shard_map(
        functools.partial(local, shape["lon"], shape["chan"], shape["lat"]),
        mesh=mesh,
        in_specs=placed,
        out_specs=(
            P("chan", ("groups", "lat"), "lon"),
            P("groups", None, "chan", None),
            P(("groups", "chan")),
        ),
        check_vma=False,
    )
```

time: 178 us -> 56.7 us (0.32)
  waiting for transfers between devices: 95.8 us -> 0 us
  Pallas kernels: 0 us -> 51.1 us
  blocking collectives: 17.9 us -> 0 us
  local copies, waits for them, and re-layouts: 19.5 us -> 3.68 us
  matrix products: 15 us -> 0 us
  between operations: 14.2 us -> 0.66 us
  starting transfers between devices: 10.5 us -> 0 us
  other arithmetic: 4.73 us -> 1.12 us
    psum x1 -> x0, waiting for transfers between devices: 60.5 us -> none  [local(): weight_grad, bias_grad = lax.psum((weight_part, bias_part), ('lon', 'lat'))]
    pallas_call x0 -> x1, Pallas kernels: none -> 51.1 us  [local(): pl.pallas_call(functools.partial(kernel, sizes), out_shape=(jax.ShapeDtyp...]
    all_gather x1 -> x0, waiting for transfers between devices: 23.9 us -> none  [local(): input_all = lax.all_gather(input_pad, 'chan', axis=0, tiled=True)]
    psum x1 -> x0, blocking collectives: 17.9 us -> none  [local(): weight_grad, bias_grad = lax.psum((weight_part, bias_part), ('lon', 'lat'))]
    dot_general x27 -> x0, matrix products: 15 us -> none  [the longest x9 5.76 us: local(): lax.dot_general(grad_pre, window, (((1,), (1,)), ((), ())), preferred_ele...]
    ppermute x8 -> x0, starting transfers between devices: 10.2 us -> none  [the longest x4 5.42 us: padded_2(): after = lax.ppermute(initial, axis, down)]
    slice x4 -> x0, local copies, waits for them, and re-layouts: 9.27 us -> none  [the longest x2 9.24 us: window_of(): field[:, first_row:first_row + row_count, first_col:first_col + column_co...]
    reduce_scatter x1 -> x0, waiting for transfers between devices: 6.31 us -> none  [local(): lax.psum_scatter(summed.reshape(amount, row_count, column_count), 'chan',...]
  transfers between devices with their start and end apart: 11 -> 0, of which waited for: 9 -> 0; matrix products, arithmetic and copies ran while one was open for 6% -> 0% of each run, Pallas kernels for 0% -> 0%
where the time goes in v1:
time: 56.7 us; the launch traced here: 56.5 us
  Pallas kernels  51.1 us (90%)
  local copies, waits for them, and re-layouts  3.68 us (6%)
  other arithmetic  1.12 us (2%)
  between operations  0.66 us (1%)
    pallas_call x1, Pallas kernels, local(): pl.pallas_call(functools.partial(kernel, sizes), out_shape=(jax.ShapeDtyp...  51.1 us
    reshape x1, local copies, waits for them, and re-layouts, local(): cotangent.reshape(C, L)  1.44 us

profile of v1, /device:TPU:0, one launch (start us, length us, event | category | flops | bytes accessed | tf_op | source)
XLA Modules:
  0.0 56.5 jit_solution(13564377884260882217)
XLA Ops:
  0.6 0.0 copy-start
  0.6 0.8 %copy.7.b_ref = f32[128,1]{1,0:T(8,128)S(1)} copy(f32[128,1]{0,1:T(1,128)} %bitcast.20) | data formatting | bytes 1024 | tf_op jit(solution)/shard_map/reshape | solution.py:352
  1.5 1.4 %copy_bitcast_fusion = (bf16[128,2048]{1,0:T(8,128)(2,1)S(1)}, bf16[128,2048]{1,0:T(8,128)(2,1)S(1)}) fusion(bf16[16,8,16,128]{3,2,1,0:T(8,128)(2,1)} %bitcast.18, bf16[16,8,16,128]{3,2,1,0:T(8,128)(2,1)} %bitcast.19), kind=kLoop, calls=%fused_computation | loop fusion | bytes 2097152 | tf_op jit(solution)/shard_map/reshape | solution.py:350
  2.9 0.0 copy-done
  2.9 51.1 %conv_backward.1 = (bf16[128,2048]{1,0:T(8,128)(2,1)S(1)}, bf16[1152,256]{1,0:T(8,128)(2,1)S(1)}, f32[8,128]{1,0:T(8,128)S(1)}) custom-call(bf16[128,2048]{1,0:T(8,128)(2,1)S(1)} %get-tuple-element.10.x_ref, bf16[128,2048]{1,0:T(8,128)(2,1)S(1)} %get-tuple-element.9.ct_ref, bf16[1152,256]{1,0:T(8,128)(2,1)S(1)} %bitcast.16, f32[128,1]{1,0:T(8,128)S(1)} %copy.7.b_ref), custom_call_target="tpu_custom_call" | custom-call | flops 3623878656 | bytes 2097152 | tf_op jit(solution)/shard_map/conv_backward/pallas_call | solution.py:298
  54.0 0.9 %copy.10 = bf16[16,8,16,128]{3,2,1,0:T(8,128)(2,1)} copy(bf16[16,8,16,128]{3,1,2,0:T(8,128)(2,1)S(1)} %bitcast.15) | data formatting | bytes 1048576
  54.9 0.5 slice_bitcast_fusion
  55.4 1.1 %convert.1 = f32[3,3,128,256]{3,2,1,0:T(8,128)} convert(bf16[3,3,128,256]{3,2,1,0:T(8,128)(2,1)S(1)} %bitcast.14) | non-fusion elementwise | flops 294912 | bytes 1769472 | tf_op jit(solution)/shard_map/reshape | solution.py:354
Async XLA Ops:
  0.6 2.3 %copy-start = (bf16[3,3,128,256]{3,2,1,0:T(8,128)(2,1)S(1)}, bf16[3,3,128,256]{3,2,1,0:T(8,128)(2,1)}, u32[]{:S(2)}) copy-start(bf16[3,3,128,256]{3,2,1,0:T(8,128)(2,1)} %param.6) | copy-start | bytes 1769476

commit v2 on v1

v2 whole, which is shorter than its diff:
```python
import functools

import jax
import jax.numpy as jnp
from jax import lax
from jax.experimental import pallas as pl
from jax.experimental.pallas import tpu as pltpu
from jax.sharding import PartitionSpec as P

MESH = pl.DeviceIdType.MESH
BF = jnp.bfloat16
F32 = jnp.float32
PIECES = 4


def gelu_slope(preact):
    normal_cdf = 0.5 * (1.0 + lax.erf(preact * 0.7071067811865476))
    density = jnp.exp(-0.5 * preact * preact) * 0.3989422804014327
    return normal_cdf + preact * density


def nt(a, b):
    return lax.dot_general(a, b, (((1,), (1,)), ((), ())), preferred_element_type=F32)


def kernel(
    sizes,
    x_ref, ct_ref, w_ref, b_ref,
    dx_ref, dw_ref, db_ref,
    xs, hx, hc, edge, shift, w2, wt, gs, hg, hgo, gedge,
    dwp, dwsend, dwcore, zsend, zrecv, gathered, bias, dxf, dxs, dxr,
    x_sem, row_sem, col_sem, grow_sem, gcol_sem, gother_sem, core_sem, rs_sem, ag_sem, fwd_sem, bias_sem, dx_sem,
):
    nlon, nchan, nlat, C, CA, H, W, R = sizes
    L = H * W
    group = lax.axis_index("groups")
    lon = lax.axis_index("lon")
    chan = lax.axis_index("chan")
    lat = lax.axis_index("lat")
    other = 1 - lat

    def at(a, b, c):
        return (group, a, b, c)

    def copy(src, dst, sems, index, device):
        return pltpu.make_async_remote_copy(
            src_ref=src, dst_ref=dst,
            send_sem=sems.at[(0,) + index], recv_sem=sems.at[(1,) + index],
            device_id=device, device_id_type=MESH,
        )

    everyone = nlon * nchan * nlat
    me = (lon * nchan + chan) * nlat + lat
    barrier = pltpu.get_barrier_semaphore()

    @pl.loop(1, everyone)
    def _(d):
        peer = lax.rem(me + d, everyone)
        pl.semaphore_signal(
            barrier, inc=1, device_id_type=MESH,
            device_id=at(peer // (nchan * nlat), lax.rem(peer // nlat, nchan), lax.rem(peer, nlat)),
        )

    def edges(field, start):
        rows, lanes = 2 * H, field.shape[1]
        row = lax.broadcasted_iota(jnp.int32, (rows, lanes), 0)
        lane = lax.broadcasted_iota(jnp.int32, (rows, lanes), 1) + start * W
        want = jnp.where(row < H, row * W, (row - H) * W + W - 1)
        pick = jnp.where(lane == want, 1.0, 0.0).astype(BF)
        return nt(pick, field).astype(BF)

    def walk(start, count):
        return jnp.where(lat == 1, start, H - start - count)

    def cols(row, count):
        return pl.ds(pl.multiple_of(row * W, W), count * W)

    edge[...] = edges(x_ref[...], 0)
    mine = pl.ds(pl.multiple_of(chan * C, C), C)
    xs[1, mine, pl.ds(W, L)] = x_ref[...]
    rim = cols(lat * (H + 1), 1)
    for q in range(3):
        xs[q, :, rim] = jnp.zeros((CA, W), BF)
        gs[q, :, rim] = jnp.zeros((C, W), BF)
    pl.semaphore_wait(barrier, everyone - 1)

    from_row = cols(other * (H - 1), 1)
    to_row = rim
    halo_copies = []
    for d in range(nchan):
        there = lax.rem(chan + d, nchan)
        halo_copies.append(
            copy(x_ref.at[:, from_row], xs.at[1, mine, to_row], row_sem, (d,), at(lon, there, other))
        )
        for side in range(2):
            lon_to = lax.rem(lon + (nlon - 1 if side == 0 else 1), nlon)
            for dl in range(2):
                halo_copies.append(
                    copy(
                        edge.at[pl.ds(side * H, H)],
                        hx.at[chan, pl.ds(((1 - side) * 2 + dl) * H, H)],
                        col_sem, (d, side, dl),
                        at(lon_to, there, lat if dl == 0 else other),
                    )
                )
    for c in halo_copies:
        c.start()
    step = H // PIECES
    x_starts = [0] + [step * j + 1 for j in range(1, PIECES)] + [H]
    x_copies = []
    for j in range(PIECES):
        count = x_starts[j + 1] - x_starts[j]
        row = walk(x_starts[j], count)
        x_copies.append([
            copy(
                x_ref.at[:, cols(row, count)], xs.at[1, mine, cols(row + 1, count)],
                x_sem, (d, j), at(lon, lax.rem(chan + d, nchan), lat),
            )
            for d in range(1, nchan)
        ])
        for c in x_copies[j]:
            c.start()

    @pl.loop(0, H + 2)
    def _(r):
        k = lax.broadcasted_iota(jnp.int32, (W + 128, 2 * W), 0)
        n = lax.broadcasted_iota(jnp.int32, (W + 128, 2 * W), 1)
        first = jnp.where(lat == 1, 2 * H - 1, -1000)
        last = jnp.where(lat == 0, H, -1000)
        held = jnp.where(r == 0, first, jnp.where(r == H + 1, last, r - 1))
        right = n >= W
        col = jnp.where(right, n - W, n)
        want = jnp.where(right, col + 1, col - 1)
        want = jnp.where(right & (col == W - 1), W + 2 * H + held, want)
        want = jnp.where((~right) & (col == 0), W + held, want)
        hit = jnp.where(k == want, 1.0, 0.0).astype(BF)
        shift[:, pl.ds(pl.multiple_of(r * 2 * W, 2 * W), 2 * W)] = hit

    for t in range(9):
        w2[:, pl.ds(t * CA, CA)] = w_ref[pl.ds(t * C, C), :]
    wt[...] = jnp.transpose(w_ref[...].astype(F32)).astype(BF)

    def build_shifts(field, columns, start, count):
        @pl.loop(0, count)
        def _(i):
            r = start + i
            here = cols(r, 1)
            both = jnp.concatenate([field[1, :, here], columns], axis=1)
            moved = jnp.dot(
                both, shift[:, pl.ds(pl.multiple_of(r * 2 * W, 2 * W), 2 * W)],
                preferred_element_type=F32,
            ).astype(BF)
            field[0, :, here] = moved[:, :W]
            field[2, :, here] = moved[:, W:]

    def turned(blocks):
        have = sum(b.shape[0] for b in blocks)
        full = jnp.concatenate(blocks + [jnp.zeros((128 - have, C), BF)], axis=0)
        return jnp.transpose(full.astype(F32)).astype(BF)

    for c in halo_copies:
        c.wait()
    for k in range(nchan):
        hc[pl.ds(k * C, C), :] = turned([hx[k]])

    ring = nlon * nlat
    spot = lon * nlat + lat
    group_rows = 3 * C
    half = R // 2
    quarter = half // nlon
    base = pl.multiple_of(lat * half, half)
    far = pl.ds(pl.multiple_of(other * half, half), half)
    core_copies, bias_copies, dx_copies = [], [], []
    dx_starts = [0] + [step * j - 1 for j in range(1, PIECES)] + [H]
    if R > group_rows:
        for g in range(3):
            dwp[g, pl.ds(group_rows, R - group_rows), :] = jnp.zeros((R - group_rows, CA), F32)
    for j in range(PIECES):
        final = j == PIECES - 1
        for c in x_copies[j]:
            c.wait()
        if final:
            for c in dx_copies:
                c.start()
        count = x_starts[j + 1] - x_starts[j]
        if j == 0:
            build_shifts(xs, hc[...], jnp.where(lat == 1, 0, H + 1 - count), count + 1)
        else:
            build_shifts(xs, hc[...], walk(x_starts[j], count) + 1, count)
        row = walk(j * step, step)
        stack = jnp.concatenate(
            [xs[q, :, cols(row + p, step)] for p in range(3) for q in range(3)], axis=0
        )
        preact = jnp.dot(w2[...], stack, preferred_element_type=F32) + b_ref[...]
        upstream = ct_ref[:, cols(row, step)].astype(F32)
        grad = (upstream * gelu_slope(preact)).astype(BF)
        gs[1, :, cols(row + 1, step)] = grad
        gedge[j] = edges(grad, row)
        grad_copies = []
        if j == 0:
            grad_copies.append(
                copy(gs.at[1, :, cols(other * (H - 1) + 1, 1)], gs.at[1, :, to_row], grow_sem, (0,), at(lon, chan, other))
            )
        for side in range(2):
            lon_to = lax.rem(lon + (nlon - 1 if side == 0 else 1), nlon)
            tile = gedge.at[j, pl.ds(side * H, H)]
            grad_copies.append(copy(tile, hg.at[j, 1 - side], gcol_sem, (j, side), at(lon_to, chan, lat)))
            if j == 0:
                grad_copies.append(copy(tile, hgo.at[1 - side], gother_sem, (side,), at(lon_to, chan, other)))
        for c in grad_copies:
            c.start()
        if final:
            bias[spot] = nt(jnp.ones((8, L), BF), gs[1, :, pl.ds(W, L)])
            for d in range(1, ring):
                peer = lax.rem(spot + d, ring)
                c = copy(bias.at[spot], bias.at[spot], bias_sem, (d,), at(peer // nlat, chan, lax.rem(peer, nlat)))
                c.start()
                bias_copies.append(c)
        for p in range(3):
            for q in range(3):
                here = pl.ds(q * C, C)
                more = nt(grad, xs[q, :, cols(row + p, step)])
                dwp[p, here, :] = more if j == 0 else dwp[p, here, :] + more
            if final:
                dwsend[p] = dwp[p, far, :].astype(BF)
                c = copy(dwsend.at[p], dwcore.at[p], core_sem, (p,), at(lon, chan, other))
                c.start()
                core_copies.append(c)
        for c in grad_copies:
            c.wait()
        if j == 0:
            sides = turned([hg[j, 0], hgo[0], hg[j, 1], hgo[1]])
            build_shifts(gs, sides, jnp.where(lat == 1, 0, H + 1 - step), step + 1)
        else:
            blank = jnp.zeros((H, C), BF)
            sides = turned([hg[j, 0], blank, hg[j, 1], blank])
            build_shifts(gs, sides, row + 1, step)
        count = dx_starts[j + 1] - dx_starts[j]
        row = walk(dx_starts[j], count)
        stack = jnp.concatenate(
            [gs[2 - q, :, cols(row + 2 - p, count)] for p in range(3) for q in range(3)], axis=0
        )
        whole = jnp.dot(wt[...], stack, preferred_element_type=F32)
        dxf[:, cols(row, count)] = whole
        dxs[:, cols(row, count)] = whole.astype(BF)
        for d in range(1, nchan):
            there = lax.rem(chan + d, nchan)
            theirs = pl.ds(pl.multiple_of(there * C, C), C)
            c = copy(
                dxs.at[theirs, cols(row, count)], dxr.at[d, :, cols(row, count)],
                dx_sem, (d, j), at(lon, there, lat),
            )
            if final:
                c.start()
            dx_copies.append(c)

    rs_copies = []
    for g in range(3):
        core_copies[g].wait()
        summed = dwp[g, pl.ds(base, half), :] + dwcore[g].astype(F32)
        dwp[g, pl.ds(base, half), :] = summed
        zsend[g] = summed.astype(BF)
        rs_copies.append([])
        for d in range(1, nlon):
            there = lax.rem(lon + d, nlon)
            c = copy(
                zsend.at[g, pl.ds(pl.multiple_of(there * quarter, 16), quarter), :],
                zrecv.at[g, d], rs_sem, (g, d), at(there, chan, lat),
            )
            c.start()
            rs_copies[g].append(c)
    own_rows = pl.ds(pl.multiple_of(base + lon * quarter, 16), quarter)
    ag_copies, fwd_copies = [], []
    for g in range(3):
        total = dwp[g, own_rows, :]
        for d in range(1, nlon):
            rs_copies[g][d - 1].wait()
            total = total + zrecv[g, d].astype(F32)
        gathered[g, own_rows, :] = total.astype(BF)
        ag_copies.append([])
        for d in range(1, nlon):
            c = copy(
                gathered.at[g, own_rows, :], gathered.at[g, own_rows, :], ag_sem, (g, d),
                at(lax.rem(lon + d, nlon), chan, lat),
            )
            c.start()
            ag_copies[g].append(c)

    def finish_dx(j):
        count = dx_starts[j + 1] - dx_starts[j]
        here = cols(walk(dx_starts[j], count), count)
        acc = dxf[mine, here]
        for d in range(1, nchan):
            dx_copies[j * (nchan - 1) + d - 1].wait()
            acc = acc + dxr[d, :, here].astype(F32)
        dx_ref[:, here] = acc.astype(BF)

    for j in range(PIECES - 1):
        finish_dx(j)
    for g in range(3):
        for d in range(nlon):
            if d > 0:
                ag_copies[g][d - 1].wait()
            source = lax.rem(lon + nlon - d, nlon)
            rows = pl.ds(pl.multiple_of(base + source * quarter, 16), quarter)
            c = copy(gathered.at[g, rows, :], gathered.at[g, rows, :], fwd_sem, (g, d), at(lon, chan, other))
            c.start()
            fwd_copies.append(c)
    finish_dx(PIECES - 1)
    for c in bias_copies:
        c.wait()
    db_ref[...] = jnp.sum(bias[...], axis=0)
    for c in fwd_copies:
        c.wait()
    dw_ref[...] = gathered[...]


def local(nlon, nchan, nlat, inputs, cotangent, weight, bias_vector):
    C, H, W = inputs.shape
    CA = weight.shape[3]
    L = H * W
    step = nlat * nlon * 16
    R = -(-3 * C // step) * step
    half = R // nlat
    sizes = (nlon, nchan, nlat, C, CA, H, W, R)
    wide = (H + 2) * W
    vmem = pl.BlockSpec(memory_space=pltpu.VMEM)
    dma = pltpu.SemaphoreType.DMA
    dx, dw, db = pl.pallas_call(
        functools.partial(kernel, sizes),
        out_shape=(
            jax.ShapeDtypeStruct((C, L), BF),
            jax.ShapeDtypeStruct((3, R, CA), BF),
            jax.ShapeDtypeStruct((8, C), F32),
        ),
        in_specs=[vmem] * 4,
        out_specs=(vmem,) * 3,
        scratch_shapes=[
            pltpu.VMEM((3, CA, wide), BF),
            pltpu.VMEM((nchan, 4 * H, C), BF),
            pltpu.VMEM((CA, 128), BF),
            pltpu.VMEM((2 * H, C), BF),
            pltpu.VMEM((W + 128, (H + 2) * 2 * W), BF),
            pltpu.VMEM((C, 9 * CA), BF),
            pltpu.VMEM((CA, 9 * C), BF),
            pltpu.VMEM((3, C, wide), BF),
            pltpu.VMEM((PIECES, 2, H, C), BF),
            pltpu.VMEM((2, H, C), BF),
            pltpu.VMEM((PIECES, 2 * H, C), BF),
            pltpu.VMEM((3, R, CA), F32),
            pltpu.VMEM((3, half, CA), BF),
            pltpu.VMEM((3, half, CA), BF),
            pltpu.VMEM((3, half, CA), BF),
            pltpu.VMEM((3, nlon, half // nlon, CA), BF),
            pltpu.VMEM((3, R, CA), BF),
            pltpu.VMEM((nlon * nlat, 8, C), F32),
            pltpu.VMEM((CA, L), F32),
            pltpu.VMEM((CA, L), BF),
            pltpu.VMEM((nchan, C, L), BF),
            dma((2, nchan, PIECES)),
            dma((2, nchan)),
            dma((2, nchan, 2, 2)),
            dma((2, 1)),
            dma((2, PIECES, 2)),
            dma((2, 2)),
            dma((2, 3)),
            dma((2, 3, nlon)),
            dma((2, 3, nlon)),
            dma((2, 3, nlon)),
            dma((2, nlon * nlat)),
            dma((2, nchan, PIECES)),
        ],
        compiler_params=pltpu.CompilerParams(
            collective_id=0, has_side_effects=True, vmem_limit_bytes=48 * 1024 * 1024
        ),
        cost_estimate=pl.CostEstimate(
            flops=3 * 2 * 9 * C * CA * L, bytes_accessed=4 * C * L * 2, transcendentals=2 * C * L
        ),
        name="conv_backward",
    )(
        inputs.reshape(C, L),
        cotangent.reshape(C, L),
        weight.reshape(9 * C, CA),
        bias_vector.reshape(C, 1),
    )
    weight_grad = dw[:, : 3 * C].astype(F32).reshape(3, 3, C, CA)
    return dx.reshape(C, H, W), weight_grad, db[0]


def solution(mesh):
    shape = mesh.shape
    placed = (
        P("chan", ("groups", "lat"), "lon"),
        P("chan", ("groups", "lat"), "lon"),
        P(None, None, "chan", None),
        P("chan"),
    )
    return jax.shard_map(
        functools.partial(local, shape["lon"], shape["chan"], shape["lat"]),
        mesh=mesh,
        in_specs=placed,
        out_specs=(
            P("chan", ("groups", "lat"), "lon"),
            P("groups", None, "chan", None),
            P(("groups", "chan")),
        ),
        check_vma=False,
    )
```

time: 56.7 us -> 58.8 us (1.037)
  Pallas kernels: 51.1 us -> 53.2 us
    pallas_call x1, Pallas kernels: 51.1 us -> 53.2 us  [local(): pl.pallas_call(functools.partial(kernel, sizes), out_shape=(jax.ShapeDtyp...]
where the time goes in v2:
time: 58.8 us; the launch traced here: 58.6 us
  Pallas kernels  53.2 us (90%)
  local copies, waits for them, and re-layouts  3.68 us (6%)
  other arithmetic  1.12 us (2%)
  between operations  0.66 us (1%)
    pallas_call x1, Pallas kernels, local(): pl.pallas_call(functools.partial(kernel, sizes), out_shape=(jax.ShapeDtyp...  53.2 us
    reshape x1, local copies, waits for them, and re-layouts, local(): cotangent.reshape(C, L)  1.44 us

profile of v2, /device:TPU:0, one launch (start us, length us, event | category | flops | bytes accessed | tf_op | source)
XLA Modules:
  0.0 58.6 jit_solution(2496207332093011474)
XLA Ops:
  0.6 0.0 copy-start
  0.6 0.8 %copy.7.b_ref = f32[128,1]{1,0:T(8,128)S(1)} copy(f32[128,1]{0,1:T(1,128)} %bitcast.20) | data formatting | bytes 1024 | tf_op jit(solution)/shard_map/reshape | solution.py:384
  1.5 1.4 %copy_bitcast_fusion = (bf16[128,2048]{1,0:T(8,128)(2,1)S(1)}, bf16[128,2048]{1,0:T(8,128)(2,1)S(1)}) fusion(bf16[16,8,16,128]{3,2,1,0:T(8,128)(2,1)} %bitcast.18, bf16[16,8,16,128]{3,2,1,0:T(8,128)(2,1)} %bitcast.19), kind=kLoop, calls=%fused_computation | loop fusion | bytes 2097152 | tf_op jit(solution)/shard_map/reshape | solution.py:382
  2.9 0.0 copy-done
  2.9 53.2 %conv_backward.1 = (bf16[128,2048]{1,0:T(8,128)(2,1)S(1)}, bf16[3,384,256]{2,1,0:T(8,128)(2,1)S(1)}, f32[8,128]{1,0:T(8,128)S(1)}) custom-call(bf16[128,2048]{1,0:T(8,128)(2,1)S(1)} %get-tuple-element.10.x_ref, bf16[128,2048]{1,0:T(8,128)(2,1)S(1)} %get-tuple-element.9.ct_ref, bf16[1152,256]{1,0:T(8,128)(2,1)S(1)} %bitcast.16, f32[128,1]{1,0:T(8,128)S(1)} %copy.7.b_ref), custom_call_target="tpu_custom_call" | custom-call | flops 3623878656 | bytes 2097152 | tf_op jit(solution)/shard_map/conv_backward/pallas_call | solution.py:329
  56.1 0.9 %copy.10 = bf16[16,8,16,128]{3,2,1,0:T(8,128)(2,1)} copy(bf16[16,8,16,128]{3,1,2,0:T(8,128)(2,1)S(1)} %bitcast.15) | data formatting | bytes 1048576
  57.0 0.5 slice_bitcast_fusion
  57.5 1.1 %convert.1 = f32[3,3,128,256]{3,2,1,0:T(8,128)} convert(bf16[3,3,128,256]{3,2,1,0:T(8,128)(2,1)S(1)} %bitcast.14) | non-fusion elementwise | flops 294912 | bytes 1769472 | tf_op jit(solution)/shard_map/reshape | solution.py:386
Async XLA Ops:
  0.6 2.3 %copy-start = (bf16[3,3,128,256]{3,2,1,0:T(8,128)(2,1)S(1)}, bf16[3,3,128,256]{3,2,1,0:T(8,128)(2,1)}, u32[]{:S(2)}) copy-start(bf16[3,3,128,256]{3,2,1,0:T(8,128)(2,1)} %param.6) | copy-start | bytes 1769476

commit v3 on v2

--- a/solution.py
+++ b/solution.py
@@ -27,7 +27,7 @@
     sizes,
     x_ref, ct_ref, w_ref, b_ref,
     dx_ref, dw_ref, db_ref,
-    xs, hx, hc, edge, shift, w2, wt, gs, hg, hgo, gedge,
+    xs, hx, hc, edge, w2, wt, gs, hg, hgo, gedge,
     dwp, dwsend, dwcore, zsend, zrecv, gathered, bias, dxf, dxs, dxr,
     x_sem, row_sem, col_sem, grow_sem, gcol_sem, gother_sem, core_sem, rs_sem, ag_sem, fwd_sem, bias_sem, dx_sem,
 ):
@@ -121,42 +121,27 @@
         for c in x_copies[j]:
             c.start()
 
-    @pl.loop(0, H + 2)
-    def _(r):
-        k = lax.broadcasted_iota(jnp.int32, (W + 128, 2 * W), 0)
-        n = lax.broadcasted_iota(jnp.int32, (W + 128, 2 * W), 1)
-        first = jnp.where(lat == 1, 2 * H - 1, -1000)
-        last = jnp.where(lat == 0, H, -1000)
-        held = jnp.where(r == 0, first, jnp.where(r == H + 1, last, r - 1))
-        right = n >= W
-        col = jnp.where(right, n - W, n)
-        want = jnp.where(right, col + 1, col - 1)
-        want = jnp.where(right & (col == W - 1), W + 2 * H + held, want)
-        want = jnp.where((~right) & (col == 0), W + held, want)
-        hit = jnp.where(k == want, 1.0, 0.0).astype(BF)
-        shift[:, pl.ds(pl.multiple_of(r * 2 * W, 2 * W), 2 * W)] = hit
-
     for t in range(9):
         w2[:, pl.ds(t * CA, CA)] = w_ref[pl.ds(t * C, C), :]
-    wt[...] = jnp.transpose(w_ref[...].astype(F32)).astype(BF)
+    wt[...] = jnp.transpose(w_ref[...])
+    bias_col = jnp.transpose(jnp.broadcast_to(b_ref[...], (128, C)))[:, :1]
 
     def build_shifts(field, columns, start, count):
-        @pl.loop(0, count)
-        def _(i):
+        lane = lax.broadcasted_iota(jnp.int32, columns.shape, 1)
+        for i in range(count):
             r = start + i
             here = cols(r, 1)
-            both = jnp.concatenate([field[1, :, here], columns], axis=1)
-            moved = jnp.dot(
-                both, shift[:, pl.ds(pl.multiple_of(r * 2 * W, 2 * W), 2 * W)],
-                preferred_element_type=F32,
-            ).astype(BF)
-            field[0, :, here] = moved[:, :W]
-            field[2, :, here] = moved[:, W:]
+            held = jnp.where(r == 0, 2 * H - 1, jnp.where(r == H + 1, H, r - 1))
+            row = field[1, :, here]
+            left = pltpu.roll(columns, lax.rem(W - held, W), 1)
+            right = pltpu.roll(columns, lax.rem(2 * W - 1 - 2 * H - held, W), 1)
+            field[0, :, here] = jnp.where(lane == 0, left, pltpu.roll(row, 1, 1))
+            field[2, :, here] = jnp.where(lane == W - 1, right, pltpu.roll(row, W - 1, 1))
 
     def turned(blocks):
         have = sum(b.shape[0] for b in blocks)
         full = jnp.concatenate(blocks + [jnp.zeros((128 - have, C), BF)], axis=0)
-        return jnp.transpose(full.astype(F32)).astype(BF)
+        return jnp.transpose(full)
 
     for c in halo_copies:
         c.wait()
@@ -191,7 +176,7 @@
         stack = jnp.concatenate(
             [xs[q, :, cols(row + p, step)] for p in range(3) for q in range(3)], axis=0
         )
-        preact = jnp.dot(w2[...], stack, preferred_element_type=F32) + b_ref[...]
+        preact = jnp.dot(w2[...], stack, preferred_element_type=F32) + bias_col
         upstream = ct_ref[:, cols(row, step)].astype(F32)
         grad = (upstream * gelu_slope(preact)).astype(BF)
         gs[1, :, cols(row + 1, step)] = grad
@@ -309,7 +294,7 @@
     finish_dx(PIECES - 1)
     for c in bias_copies:
         c.wait()
-    db_ref[...] = jnp.sum(bias[...], axis=0)
+    db_ref[...] = jnp.sum(bias[...], axis=0)[:1]
     for c in fwd_copies:
         c.wait()
     dw_ref[...] = gathered[...]
@@ -331,7 +316,7 @@
         out_shape=(
             jax.ShapeDtypeStruct((C, L), BF),
             jax.ShapeDtypeStruct((3, R, CA), BF),
-            jax.ShapeDtypeStruct((8, C), F32),
+            jax.ShapeDtypeStruct((1, C), F32),
         ),
         in_specs=[vmem] * 4,
         out_specs=(vmem,) * 3,
@@ -340,7 +325,6 @@
             pltpu.VMEM((nchan, 4 * H, C), BF),
             pltpu.VMEM((CA, 128), BF),
             pltpu.VMEM((2 * H, C), BF),
-            pltpu.VMEM((W + 128, (H + 2) * 2 * W), BF),
             pltpu.VMEM((C, 9 * CA), BF),
             pltpu.VMEM((CA, 9 * C), BF),
             pltpu.VMEM((3, C, wide), BF),
@@ -381,10 +365,10 @@
         inputs.reshape(C, L),
         cotangent.reshape(C, L),
         weight.reshape(9 * C, CA),
-        bias_vector.reshape(C, 1),
+        bias_vector.reshape(1, C),
     )
     weight_grad = dw[:, : 3 * C].astype(F32).reshape(3, 3, C, CA)
-    return dx.reshape(C, H, W), weight_grad, db[0]
+    return dx.reshape(C, H, W), weight_grad, db.reshape(C)
 
 
 def solution(mesh):

time: 58.8 us -> 53.8 us (0.915)
  Pallas kernels: 53.2 us -> 48.9 us
  local copies, waits for them, and re-layouts: 3.68 us -> 2.92 us
    pallas_call x1, Pallas kernels: 53.2 us -> 48.9 us  [local(): pl.pallas_call(functools.partial(kernel, sizes), out_shape=(jax.ShapeDtyp...]
    reshape x1 -> x0, local copies, waits for them, and re-layouts: 0.82 us -> none  [local(): bias_vector.reshape(C, 1)]
    unnamed x3 -> x6, local copies, waits for them, and re-layouts: 0.91 us -> 1.42 us
where the time goes in v3:
time: 53.8 us; the launch traced here: 53.7 us
  Pallas kernels  48.9 us (91%)
  local copies, waits for them, and re-layouts  2.92 us (5%)
  other arithmetic  1.13 us (2%)
  between operations  0.67 us (1%)
    pallas_call x1, Pallas kernels, local(): pl.pallas_call(functools.partial(kernel, sizes), out_shape=(jax.ShapeDtyp...  48.9 us
    reshape x1, local copies, waits for them, and re-layouts, local(): cotangent.reshape(C, L)  1.5 us
    unnamed x6, local copies, waits for them, and re-layouts  1.42 us
    reshape x1, other arithmetic, local(): weight_grad = dw[:, :3 * C].astype(F32).reshape(3, 3, C, CA)  1.13 us

profile of v3, /device:TPU:0, one launch (start us, length us, event | category | flops | bytes accessed | tf_op | source)
XLA Modules:
  0.0 53.7 jit_solution(14753891566762728572)
XLA Ops:
  0.6 0.0 copy-start.1
  0.6 0.0 copy-start
  0.7 1.5 %copy_bitcast_fusion = (bf16[128,2048]{1,0:T(8,128)(2,1)S(1)}, bf16[128,2048]{1,0:T(8,128)(2,1)S(1)}) fusion(bf16[16,8,16,128]{3,2,1,0:T(8,128)(2,1)} %bitcast.19, bf16[16,8,16,128]{3,2,1,0:T(8,128)(2,1)} %bitcast.20), kind=kLoop, calls=%fused_computation | loop fusion | bytes 2097152 | tf_op jit(solution)/shard_map/reshape | solution.py:366
  2.2 0.0 copy-done.1
  2.2 0.0 copy-done
  2.2 48.9 %conv_backward.1 = (bf16[128,2048]{1,0:T(8,128)(2,1)S(1)}, bf16[3,384,256]{2,1,0:T(8,128)(2,1)S(1)}, f32[1,128]{1,0:T(1,128)S(1)}) custom-call(bf16[128,2048]{1,0:T(8,128)(2,1)S(1)} %get-tuple-element.10.x_ref, bf16[128,2048]{1,0:T(8,128)(2,1)S(1)} %get-tuple-element.9.ct_ref, bf16[1152,256]{1,0:T(8,128)(2,1)S(1)} %bitcast.15, f32[1,128]{1,0:T(1,128)S(1)} %bitcast.16), custom_call_target="tpu_custom_call" | custom-call | flops 3623878656 | bytes 2097152 | tf_op jit(solution)/shard_map/conv_backward/pallas_call | solution.py:314
  51.1 0.9 %copy.9 = bf16[16,8,16,128]{3,2,1,0:T(8,128)(2,1)} copy(bf16[16,8,16,128]{3,1,2,0:T(8,128)(2,1)S(1)} %bitcast.14) | data formatting | bytes 1048576
  52.0 1.1 %convert.1 = f32[3,3,128,256]{3,2,1,0:T(8,128)} convert(bf16[3,3,128,256]{3,2,1,0:T(8,128)(2,1)S(1)} %bitcast.13) | non-fusion elementwise | flops 294912 | bytes 1769472 | tf_op jit(solution)/shard_map/reshape | solution.py:370
  53.2 0.5 copy.13
Async XLA Ops:
  0.6 1.5 %copy-start.1 = (f32[128]{0:T(128)S(1)}, f32[128]{0:T(128)}, u32[]{:S(2)}) copy-start(f32[128]{0:T(128)} %param.7) | copy-start | bytes 1540
  0.6 1.5 %copy-start = (bf16[3,3,128,256]{3,2,1,0:T(8,128)(2,1)S(1)}, bf16[3,3,128,256]{3,2,1,0:T(8,128)(2,1)}, u32[]{:S(2)}) copy-start(bf16[3,3,128,256]{3,2,1,0:T(8,128)(2,1)} %param.6) | copy-start | bytes 1769476

commit v4 on v3

--- a/solution.py
+++ b/solution.py
@@ -160,6 +160,38 @@
     if R > group_rows:
         for g in range(3):
             dwp[g, pl.ds(group_rows, R - group_rows), :] = jnp.zeros((R - group_rows, CA), F32)
+    pending = []
+
+    def input_grad(j, send):
+        grad_copies, row = pending[j]
+        for c in grad_copies:
+            c.wait()
+        if j == 0:
+            sides = turned([hg[j, 0], hgo[0], hg[j, 1], hgo[1]])
+            build_shifts(gs, sides, jnp.where(lat == 1, 0, H + 1 - step), step + 1)
+        else:
+            blank = jnp.zeros((H, C), BF)
+            sides = turned([hg[j, 0], blank, hg[j, 1], blank])
+            build_shifts(gs, sides, row + 1, step)
+        count = dx_starts[j + 1] - dx_starts[j]
+        row = walk(dx_starts[j], count)
+        stack = jnp.concatenate(
+            [gs[2 - q, :, cols(row + 2 - p, count)] for p in range(3) for q in range(3)], axis=0
+        )
+        whole = jnp.dot(wt[...], stack, preferred_element_type=F32)
+        dxf[:, cols(row, count)] = whole
+        dxs[:, cols(row, count)] = whole.astype(BF)
+        for d in range(1, nchan):
+            there = lax.rem(chan + d, nchan)
+            theirs = pl.ds(pl.multiple_of(there * C, C), C)
+            c = copy(
+                dxs.at[theirs, cols(row, count)], dxr.at[d, :, cols(row, count)],
+                dx_sem, (d, j), at(lon, there, lat),
+            )
+            if send:
+                c.start()
+            dx_copies.append(c)
+
     for j in range(PIECES):
         final = j == PIECES - 1
         for c in x_copies[j]:
@@ -194,13 +226,6 @@
                 grad_copies.append(copy(tile, hgo.at[1 - side], gother_sem, (side,), at(lon_to, chan, other)))
         for c in grad_copies:
             c.start()
-        if final:
-            bias[spot] = nt(jnp.ones((8, L), BF), gs[1, :, pl.ds(W, L)])
-            for d in range(1, ring):
-                peer = lax.rem(spot + d, ring)
-                c = copy(bias.at[spot], bias.at[spot], bias_sem, (d,), at(peer // nlat, chan, lax.rem(peer, nlat)))
-                c.start()
-                bias_copies.append(c)
         for p in range(3):
             for q in range(3):
                 here = pl.ds(q * C, C)
@@ -211,33 +236,9 @@
                 c = copy(dwsend.at[p], dwcore.at[p], core_sem, (p,), at(lon, chan, other))
                 c.start()
                 core_copies.append(c)
-        for c in grad_copies:
-            c.wait()
-        if j == 0:
-            sides = turned([hg[j, 0], hgo[0], hg[j, 1], hgo[1]])
-            build_shifts(gs, sides, jnp.where(lat == 1, 0, H + 1 - step), step + 1)
-        else:
-            blank = jnp.zeros((H, C), BF)
-            sides = turned([hg[j, 0], blank, hg[j, 1], blank])
-            build_shifts(gs, sides, row + 1, step)
-        count = dx_starts[j + 1] - dx_starts[j]
-        row = walk(dx_starts[j], count)
-        stack = jnp.concatenate(
-            [gs[2 - q, :, cols(row + 2 - p, count)] for p in range(3) for q in range(3)], axis=0
-        )
-        whole = jnp.dot(wt[...], stack, preferred_element_type=F32)
-        dxf[:, cols(row, count)] = whole
-        dxs[:, cols(row, count)] = whole.astype(BF)
-        for d in range(1, nchan):
-            there = lax.rem(chan + d, nchan)
-            theirs = pl.ds(pl.multiple_of(there * C, C), C)
-            c = copy(
-                dxs.at[theirs, cols(row, count)], dxr.at[d, :, cols(row, count)],
-                dx_sem, (d, j), at(lon, there, lat),
-            )
-            if final:
-                c.start()
-            dx_copies.append(c)
+        pending.append((grad_copies, row))
+        if j > 0:
+            input_grad(j - 1, final)
 
     rs_copies = []
     for g in range(3):
@@ -254,6 +255,13 @@
             )
             c.start()
             rs_copies[g].append(c)
+    input_grad(PIECES - 1, True)
+    bias[spot] = nt(jnp.ones((8, L), BF), gs[1, :, pl.ds(W, L)])
+    for d in range(1, ring):
+        peer = lax.rem(spot + d, ring)
+        c = copy(bias.at[spot], bias.at[spot], bias_sem, (d,), at(peer // nlat, chan, lax.rem(peer, nlat)))
+        c.start()
+        bias_copies.append(c)
     own_rows = pl.ds(pl.multiple_of(base + lon * quarter, 16), quarter)
     ag_copies, fwd_copies = [], []
     for g in range(3):

time: 53.8 us -> 47.5 us (0.88)
  Pallas kernels: 48.9 us -> 42.6 us
    pallas_call x1, Pallas kernels: 48.9 us -> 42.6 us  [local(): pl.pallas_call(functools.partial(kernel, sizes), out_shape=(jax.ShapeDtyp...]
where the time goes in v4:
time: 47.5 us; the launch traced here: 47.3 us
  Pallas kernels  42.6 us (90%)
  local copies, waits for them, and re-layouts  2.92 us (6%)
  other arithmetic  1.13 us (2%)
  between operations  0.67 us (1%)
    pallas_call x1, Pallas kernels, local(): pl.pallas_call(functools.partial(kernel, sizes), out_shape=(jax.ShapeDtyp...  42.6 us
    reshape x1, local copies, waits for them, and re-layouts, local(): cotangent.reshape(C, L)  1.5 us
    unnamed x6, local copies, waits for them, and re-layouts  1.42 us
    reshape x1, other arithmetic, local(): weight_grad = dw[:, :3 * C].astype(F32).reshape(3, 3, C, CA)  1.13 us

profile of v4, /device:TPU:0, one launch (start us, length us, event | category | flops | bytes accessed | tf_op | source)
XLA Modules:
  0.0 47.3 jit_solution(1892112482369435952)
XLA Ops:
  0.6 0.0 copy-start.1
  0.6 0.0 copy-start
  0.7 1.5 %copy_bitcast_fusion = (bf16[128,2048]{1,0:T(8,128)(2,1)S(1)}, bf16[128,2048]{1,0:T(8,128)(2,1)S(1)}) fusion(bf16[16,8,16,128]{3,2,1,0:T(8,128)(2,1)} %bitcast.19, bf16[16,8,16,128]{3,2,1,0:T(8,128)(2,1)} %bitcast.20), kind=kLoop, calls=%fused_computation | loop fusion | bytes 2097152 | tf_op jit(solution)/shard_map/reshape | solution.py:374
  2.2 0.0 copy-done.1
  2.2 0.0 copy-done
  2.2 42.6 %conv_backward.1 = (bf16[128,2048]{1,0:T(8,128)(2,1)S(1)}, bf16[3,384,256]{2,1,0:T(8,128)(2,1)S(1)}, f32[1,128]{1,0:T(1,128)S(1)}) custom-call(bf16[128,2048]{1,0:T(8,128)(2,1)S(1)} %get-tuple-element.10.x_ref, bf16[128,2048]{1,0:T(8,128)(2,1)S(1)} %get-tuple-element.9.ct_ref, bf16[1152,256]{1,0:T(8,128)(2,1)S(1)} %bitcast.15, f32[1,128]{1,0:T(1,128)S(1)} %bitcast.16), custom_call_target="tpu_custom_call" | custom-call | flops 3623878656 | bytes 2097152 | tf_op jit(solution)/shard_map/conv_backward/pallas_call | solution.py:322
  44.8 0.9 %copy.9 = bf16[16,8,16,128]{3,2,1,0:T(8,128)(2,1)} copy(bf16[16,8,16,128]{3,1,2,0:T(8,128)(2,1)S(1)} %bitcast.14) | data formatting | bytes 1048576
  45.7 1.1 %convert.1 = f32[3,3,128,256]{3,2,1,0:T(8,128)} convert(bf16[3,3,128,256]{3,2,1,0:T(8,128)(2,1)S(1)} %bitcast.13) | non-fusion elementwise | flops 294912 | bytes 1769472 | tf_op jit(solution)/shard_map/reshape | solution.py:378
  46.8 0.5 %copy.13 = f32[128]{0:T(128)} copy(f32[128]{0:T(128)S(1)} %bitcast.17) | data formatting | bytes 1024
Async XLA Ops:
  0.6 1.5 %copy-start.1 = (f32[128]{0:T(128)S(1)}, f32[128]{0:T(128)}, u32[]{:S(2)}) copy-start(f32[128]{0:T(128)} %param.7) | copy-start | bytes 1540
  0.6 1.5 %copy-start = (bf16[3,3,128,256]{3,2,1,0:T(8,128)(2,1)S(1)}, bf16[3,3,128,256]{3,2,1,0:T(8,128)(2,1)}, u32[]{:S(2)}) copy-start(bf16[3,3,128,256]{3,2,1,0:T(8,128)(2,1)} %param.6) | copy-start | bytes 1769476

commit v5 on v4

--- a/solution.py
+++ b/solution.py
@@ -162,7 +162,7 @@
             dwp[g, pl.ds(group_rows, R - group_rows), :] = jnp.zeros((R - group_rows, CA), F32)
     pending = []
 
-    def input_grad(j, send):
+    def input_grad(j):
         grad_copies, row = pending[j]
         for c in grad_copies:
             c.wait()
@@ -188,17 +188,13 @@
                 dxs.at[theirs, cols(row, count)], dxr.at[d, :, cols(row, count)],
                 dx_sem, (d, j), at(lon, there, lat),
             )
-            if send:
-                c.start()
+            c.start()
             dx_copies.append(c)
 
     for j in range(PIECES):
         final = j == PIECES - 1
         for c in x_copies[j]:
             c.wait()
-        if final:
-            for c in dx_copies:
-                c.start()
         count = x_starts[j + 1] - x_starts[j]
         if j == 0:
             build_shifts(xs, hc[...], jnp.where(lat == 1, 0, H + 1 - count), count + 1)
@@ -237,9 +233,8 @@
                 c.start()
                 core_copies.append(c)
         pending.append((grad_copies, row))
-        if j > 0:
-            input_grad(j - 1, final)
-
+
+    input_grad(0)
     rs_copies = []
     for g in range(3):
         core_copies[g].wait()
@@ -255,7 +250,8 @@
             )
             c.start()
             rs_copies[g].append(c)
-    input_grad(PIECES - 1, True)
+    for j in range(1, PIECES):
+        input_grad(j)
     bias[spot] = nt(jnp.ones((8, L), BF), gs[1, :, pl.ds(W, L)])
     for d in range(1, ring):
         peer = lax.rem(spot + d, ring)

time: 47.5 us -> 45.6 us (0.960)
  Pallas kernels: 42.6 us -> 40.7 us
    pallas_call x1, Pallas kernels: 42.6 us -> 40.7 us  [local(): pl.pallas_call(functools.partial(kernel, sizes), out_shape=(jax.ShapeDtyp...]
where the time goes in v5:
time: 45.6 us; the launch traced here: 45.4 us
  Pallas kernels  40.7 us (89%)
  local copies, waits for them, and re-layouts  2.92 us (6%)
  other arithmetic  1.13 us (2%)
  between operations  0.67 us (1%)
    pallas_call x1, Pallas kernels, local(): pl.pallas_call(functools.partial(kernel, sizes), out_shape=(jax.ShapeDtyp...  40.7 us
    reshape x1, local copies, waits for them, and re-layouts, local(): cotangent.reshape(C, L)  1.5 us
    unnamed x6, local copies, waits for them, and re-layouts  1.42 us
    reshape x1, other arithmetic, local(): weight_grad = dw[:, :3 * C].astype(F32).reshape(3, 3, C, CA)  1.13 us

profile of v5, /device:TPU:0, one launch (start us, length us, event | category | flops | bytes accessed | tf_op | source)
XLA Modules:
  0.0 45.4 jit_solution(16893424346492703899)
XLA Ops:
  0.6 0.0 copy-start.1
  0.6 0.0 copy-start
  0.7 1.5 %copy_bitcast_fusion = (bf16[128,2048]{1,0:T(8,128)(2,1)S(1)}, bf16[128,2048]{1,0:T(8,128)(2,1)S(1)}) fusion(bf16[16,8,16,128]{3,2,1,0:T(8,128)(2,1)} %bitcast.19, bf16[16,8,16,128]{3,2,1,0:T(8,128)(2,1)} %bitcast.20), kind=kLoop, calls=%fused_computation | loop fusion | bytes 2097152 | tf_op jit(solution)/shard_map/reshape | solution.py:370
  2.2 0.0 copy-done.1
  2.2 0.0 copy-done
  2.2 40.7 %conv_backward.1 = (bf16[128,2048]{1,0:T(8,128)(2,1)S(1)}, bf16[3,384,256]{2,1,0:T(8,128)(2,1)S(1)}, f32[1,128]{1,0:T(1,128)S(1)}) custom-call(bf16[128,2048]{1,0:T(8,128)(2,1)S(1)} %get-tuple-element.10.x_ref, bf16[128,2048]{1,0:T(8,128)(2,1)S(1)} %get-tuple-element.9.ct_ref, bf16[1152,256]{1,0:T(8,128)(2,1)S(1)} %bitcast.15, f32[1,128]{1,0:T(1,128)S(1)} %bitcast.16), custom_call_target="tpu_custom_call" | custom-call | flops 3623878656 | bytes 2097152 | tf_op jit(solution)/shard_map/conv_backward/pallas_call | solution.py:318
  42.9 0.9 %copy.9 = bf16[16,8,16,128]{3,2,1,0:T(8,128)(2,1)} copy(bf16[16,8,16,128]{3,1,2,0:T(8,128)(2,1)S(1)} %bitcast.14) | data formatting | bytes 1048576
  43.8 1.1 %convert.1 = f32[3,3,128,256]{3,2,1,0:T(8,128)} convert(bf16[3,3,128,256]{3,2,1,0:T(8,128)(2,1)S(1)} %bitcast.13) | non-fusion elementwise | flops 294912 | bytes 1769472 | tf_op jit(solution)/shard_map/reshape | solution.py:374
  44.9 0.5 %copy.13 = f32[128]{0:T(128)} copy(f32[128]{0:T(128)S(1)} %bitcast.17) | data formatting | bytes 1024
Async XLA Ops:
  0.6 1.5 %copy-start.1 = (f32[128]{0:T(128)S(1)}, f32[128]{0:T(128)}, u32[]{:S(2)}) copy-start(f32[128]{0:T(128)} %param.7) | copy-start | bytes 1540
  0.6 1.5 %copy-start = (bf16[3,3,128,256]{3,2,1,0:T(8,128)(2,1)S(1)}, bf16[3,3,128,256]{3,2,1,0:T(8,128)(2,1)}, u32[]{:S(2)}) copy-start(bf16[3,3,128,256]{3,2,1,0:T(8,128)(2,1)} %param.6) | copy-start | bytes 1769476

commit v6 on v5

--- a/solution.py
+++ b/solution.py
@@ -28,8 +28,8 @@
     x_ref, ct_ref, w_ref, b_ref,
     dx_ref, dw_ref, db_ref,
     xs, hx, hc, edge, w2, wt, gs, hg, hgo, gedge,
-    dwp, dwsend, dwcore, zsend, zrecv, gathered, bias, dxf, dxs, dxr,
-    x_sem, row_sem, col_sem, grow_sem, gcol_sem, gother_sem, core_sem, rs_sem, ag_sem, fwd_sem, bias_sem, dx_sem,
+    dwp, dwsend, dwcore, zsend, zpair, zlast, zrecv, gathered, bias, dxf, dxs, dxr,
+    x_sem, row_sem, col_sem, grow_sem, gcol_sem, gother_sem, core_sem, pair_sem, rs_sem, ag_sem, ag_pair_sem, fwd_sem, bias_sem, dx_sem,
 ):
     nlon, nchan, nlat, C, CA, H, W, R = sizes
     L = H * W
@@ -103,8 +103,6 @@
                         at(lon_to, there, lat if dl == 0 else other),
                     )
                 )
-    for c in halo_copies:
-        c.start()
     step = H // PIECES
     x_starts = [0] + [step * j + 1 for j in range(1, PIECES)] + [H]
     x_copies = []
@@ -120,6 +118,9 @@
         ])
         for c in x_copies[j]:
             c.start()
+        if j == 0:
+            for c in halo_copies:
+                c.start()
 
     for t in range(9):
         w2[:, pl.ds(t * CA, CA)] = w_ref[pl.ds(t * C, C), :]
@@ -234,46 +235,78 @@
                 core_copies.append(c)
         pending.append((grad_copies, row))
 
+    twos = nlon // 2
+    parity = lax.rem(lon, 2)
+    mate = at(lon + 1 - 2 * parity, chan, lat)
+    zone = twos * quarter
+    own_zone = pl.ds(pl.multiple_of(base + parity * zone, 16), zone)
+    mate_zone = pl.ds(pl.multiple_of(base + (1 - parity) * zone, 16), zone)
+    place = lon // 2
+    own_rows = pl.ds(pl.multiple_of(base + parity * zone + place * quarter, 16), quarter)
+
+    def peers(e):
+        there = lax.rem(place + e, twos)
+        return there, at(there * 2 + parity, chan, lat)
+
+    pair_copies, rs_copies, ag_copies, ag_pair_copies, fwd_copies = [], [], [], [], []
     input_grad(0)
-    rs_copies = []
     for g in range(3):
         core_copies[g].wait()
-        summed = dwp[g, pl.ds(base, half), :] + dwcore[g].astype(F32)
-        dwp[g, pl.ds(base, half), :] = summed
-        zsend[g] = summed.astype(BF)
+        dwp[g, pl.ds(base, half), :] = dwp[g, pl.ds(base, half), :] + dwcore[g].astype(F32)
+        zsend[g] = dwp[g, mate_zone, :].astype(BF)
+        c = copy(zsend.at[g], zpair.at[g], pair_sem, (g,), mate)
+        c.start()
+        pair_copies.append(c)
+    input_grad(1)
+    for g in range(3):
+        pair_copies[g].wait()
+        summed = dwp[g, own_zone, :] + zpair[g].astype(F32)
+        dwp[g, own_zone, :] = summed
+        zlast[g] = summed.astype(BF)
         rs_copies.append([])
-        for d in range(1, nlon):
-            there = lax.rem(lon + d, nlon)
+        for e in range(1, twos):
+            there, device = peers(e)
             c = copy(
-                zsend.at[g, pl.ds(pl.multiple_of(there * quarter, 16), quarter), :],
-                zrecv.at[g, d], rs_sem, (g, d), at(there, chan, lat),
+                zlast.at[g, pl.ds(pl.multiple_of(there * quarter, 16), quarter), :],
+                zrecv.at[g, e], rs_sem, (g, e), device,
             )
             c.start()
             rs_copies[g].append(c)
-    for j in range(1, PIECES):
+    input_grad(2)
+    for g in range(3):
+        total = dwp[g, own_rows, :]
+        for e in range(1, twos):
+            rs_copies[g][e - 1].wait()
+            total = total + zrecv[g, e].astype(F32)
+        gathered[g, own_rows, :] = total.astype(BF)
+        ag_copies.append([])
+        for e in range(1, twos):
+            c = copy(
+                gathered.at[g, own_rows, :], gathered.at[g, own_rows, :], ag_sem, (g, e), peers(e)[1]
+            )
+            c.start()
+            ag_copies[g].append(c)
+    for j in range(3, PIECES):
         input_grad(j)
+
+    def forward(g, k, rows):
+        c = copy(gathered.at[g, rows, :], gathered.at[g, rows, :], fwd_sem, (g, k), at(lon, chan, other))
+        c.start()
+        fwd_copies.append(c)
+
+    for g in range(3):
+        for c in ag_copies[g]:
+            c.wait()
+        c = copy(gathered.at[g, own_zone, :], gathered.at[g, own_zone, :], ag_pair_sem, (g,), mate)
+        c.start()
+        ag_pair_copies.append(c)
+        forward(g, 0, own_zone)
     bias[spot] = nt(jnp.ones((8, L), BF), gs[1, :, pl.ds(W, L)])
     for d in range(1, ring):
         peer = lax.rem(spot + d, ring)
         c = copy(bias.at[spot], bias.at[spot], bias_sem, (d,), at(peer // nlat, chan, lax.rem(peer, nlat)))
         c.start()
         bias_copies.append(c)
-    own_rows = pl.ds(pl.multiple_of(base + lon * quarter, 16), quarter)
-    ag_copies, fwd_copies = [], []
-    for g in range(3):
-        total = dwp[g, own_rows, :]
-        for d in range(1, nlon):
-            rs_copies[g][d - 1].wait()
-            total = total + zrecv[g, d].astype(F32)
-        gathered[g, own_rows, :] = total.astype(BF)
-        ag_copies.append([])
-        for d in range(1, nlon):
-            c = copy(
-                gathered.at[g, own_rows, :], gathered.at[g, own_rows, :], ag_sem, (g, d),
-                at(lax.rem(lon + d, nlon), chan, lat),
-            )
-            c.start()
-            ag_copies[g].append(c)
 
     def finish_dx(j):
         count = dx_starts[j + 1] - dx_starts[j]
@@ -287,14 +320,8 @@
     for j in range(PIECES - 1):
         finish_dx(j)
     for g in range(3):
-        for d in range(nlon):
-            if d > 0:
-                ag_copies[g][d - 1].wait()
-            source = lax.rem(lon + nlon - d, nlon)
-            rows = pl.ds(pl.multiple_of(base + source * quarter, 16), quarter)
-            c = copy(gathered.at[g, rows, :], gathered.at[g, rows, :], fwd_sem, (g, d), at(lon, chan, other))
-            c.start()
-            fwd_copies.append(c)
+        ag_pair_copies[g].wait()
+        forward(g, 1, mate_zone)
     finish_dx(PIECES - 1)
     for c in bias_copies:
         c.wait()
@@ -338,8 +365,10 @@
             pltpu.VMEM((3, R, CA), F32),
             pltpu.VMEM((3, half, CA), BF),
             pltpu.VMEM((3, half, CA), BF),
-            pltpu.VMEM((3, half, CA), BF),
-            pltpu.VMEM((3, nlon, half // nlon, CA), BF),
+            pltpu.VMEM((3, half // 2, CA), BF),
+            pltpu.VMEM((3, half // 2, CA), BF),
+            pltpu.VMEM((3, half // 2, CA), BF),
+            pltpu.VMEM((3, nlon // 2, half // nlon, CA), BF),
             pltpu.VMEM((3, R, CA), BF),
             pltpu.VMEM((nlon * nlat, 8, C), F32),
             pltpu.VMEM((CA, L), F32),
@@ -352,9 +381,11 @@
             dma((2, PIECES, 2)),
             dma((2, 2)),
             dma((2, 3)),
-            dma((2, 3, nlon)),
-            dma((2, 3, nlon)),
-            dma((2, 3, nlon)),
+            dma((2, 3)),
+            dma((2, 3, nlon // 2)),
+            dma((2, 3, nlon // 2)),
+            dma((2, 3)),
+            dma((2, 3, 2)),
             dma((2, nlon * nlat)),
             dma((2, nchan, PIECES)),
         ],

time: 45.6 us -> 47.6 us (1.044)
  Pallas kernels: 40.7 us -> 42.7 us
    pallas_call x1, Pallas kernels: 40.7 us -> 42.7 us  [local(): pl.pallas_call(functools.partial(kernel, sizes), out_shape=(jax.ShapeDtyp...]
where the time goes in v6:
time: 47.6 us; the launch traced here: 47.5 us
  Pallas kernels  42.7 us (90%)
  local copies, waits for them, and re-layouts  2.92 us (6%)
  other arithmetic  1.13 us (2%)
  between operations  0.67 us (1%)
    pallas_call x1, Pallas kernels, local(): pl.pallas_call(functools.partial(kernel, sizes), out_shape=(jax.ShapeDtyp...  42.7 us
    reshape x1, local copies, waits for them, and re-layouts, local(): cotangent.reshape(C, L)  1.5 us
    unnamed x6, local copies, waits for them, and re-layouts  1.42 us
    reshape x1, other arithmetic, local(): weight_grad = dw[:, :3 * C].astype(F32).reshape(3, 3, C, CA)  1.13 us

profile of v6, /device:TPU:0, one launch (start us, length us, event | category | flops | bytes accessed | tf_op | source)
XLA Modules:
  0.0 47.5 jit_solution(5537352902082007678)
XLA Ops:
  0.6 0.0 copy-start.1
  0.6 0.0 copy-start
  0.7 1.5 %copy_bitcast_fusion = (bf16[128,2048]{1,0:T(8,128)(2,1)S(1)}, bf16[128,2048]{1,0:T(8,128)(2,1)S(1)}) fusion(bf16[16,8,16,128]{3,2,1,0:T(8,128)(2,1)} %bitcast.19, bf16[16,8,16,128]{3,2,1,0:T(8,128)(2,1)} %bitcast.20), kind=kLoop, calls=%fused_computation | loop fusion | bytes 2097152 | tf_op jit(solution)/shard_map/reshape | solution.py:401
  2.2 0.0 copy-done.1
  2.2 0.0 copy-done
  2.2 42.7 %conv_backward.1 = (bf16[128,2048]{1,0:T(8,128)(2,1)S(1)}, bf16[3,384,256]{2,1,0:T(8,128)(2,1)S(1)}, f32[1,128]{1,0:T(1,128)S(1)}) custom-call(bf16[128,2048]{1,0:T(8,128)(2,1)S(1)} %get-tuple-element.10.x_ref, bf16[128,2048]{1,0:T(8,128)(2,1)S(1)} %get-tuple-element.9.ct_ref, bf16[1152,256]{1,0:T(8,128)(2,1)S(1)} %bitcast.15, f32[1,128]{1,0:T(1,128)S(1)} %bitcast.16), custom_call_target="tpu_custom_call" | custom-call | flops 3623878656 | bytes 2097152 | tf_op jit(solution)/shard_map/conv_backward/pallas_call | solution.py:345
  44.9 0.9 %copy.9 = bf16[16,8,16,128]{3,2,1,0:T(8,128)(2,1)} copy(bf16[16,8,16,128]{3,1,2,0:T(8,128)(2,1)S(1)} %bitcast.14) | data formatting | bytes 1048576
  45.8 1.1 %convert.1 = f32[3,3,128,256]{3,2,1,0:T(8,128)} convert(bf16[3,3,128,256]{3,2,1,0:T(8,128)(2,1)S(1)} %bitcast.13) | non-fusion elementwise | flops 294912 | bytes 1769472 | tf_op jit(solution)/shard_map/reshape | solution.py:405
  47.0 0.5 %copy.13 = f32[128]{0:T(128)} copy(f32[128]{0:T(128)S(1)} %bitcast.17) | data formatting | bytes 1024
Async XLA Ops:
  0.6 1.5 %copy-start.1 = (f32[128]{0:T(128)S(1)}, f32[128]{0:T(128)}, u32[]{:S(2)}) copy-start(f32[128]{0:T(128)} %param.7) | copy-start | bytes 1540
  0.6 1.5 %copy-start = (bf16[3,3,128,256]{3,2,1,0:T(8,128)(2,1)S(1)}, bf16[3,3,128,256]{3,2,1,0:T(8,128)(2,1)}, u32[]{:S(2)}) copy-start(bf16[3,3,128,256]{3,2,1,0:T(8,128)(2,1)} %param.6) | copy-start | bytes 1769476

commit v7 on v5

--- a/solution.py
+++ b/solution.py
@@ -105,8 +105,8 @@
                 )
     for c in halo_copies:
         c.start()
-    step = H // PIECES
-    x_starts = [0] + [step * j + 1 for j in range(1, PIECES)] + [H]
+    g_starts = [H * k // 16 for k in (0, 4, 8, 12, 16)]
+    x_starts = [0] + [k + 1 for k in g_starts[1:-1]] + [H]
     x_copies = []
     for j in range(PIECES):
         count = x_starts[j + 1] - x_starts[j]
@@ -126,27 +126,42 @@
     wt[...] = jnp.transpose(w_ref[...])
     bias_col = jnp.transpose(jnp.broadcast_to(b_ref[...], (128, C)))[:, :1]
 
-    def build_shifts(field, columns, start, count):
+    def build_shifts(field, who, columns, start, count):
         lane = lax.broadcasted_iota(jnp.int32, columns.shape, 1)
         for i in range(count):
             r = start + i
             here = cols(r, 1)
             held = jnp.where(r == 0, 2 * H - 1, jnp.where(r == H + 1, H, r - 1))
-            row = field[1, :, here]
+            row = field[1, who, here]
             left = pltpu.roll(columns, lax.rem(W - held, W), 1)
             right = pltpu.roll(columns, lax.rem(2 * W - 1 - 2 * H - held, W), 1)
-            field[0, :, here] = jnp.where(lane == 0, left, pltpu.roll(row, 1, 1))
-            field[2, :, here] = jnp.where(lane == W - 1, right, pltpu.roll(row, W - 1, 1))
+            field[0, who, here] = jnp.where(lane == 0, left, pltpu.roll(row, 1, 1))
+            field[2, who, here] = jnp.where(lane == W - 1, right, pltpu.roll(row, W - 1, 1))
 
     def turned(blocks):
         have = sum(b.shape[0] for b in blocks)
         full = jnp.concatenate(blocks + [jnp.zeros((128 - have, C), BF)], axis=0)
         return jnp.transpose(full)
 
-    for c in halo_copies:
-        c.wait()
-    for k in range(nchan):
-        hc[pl.ds(k * C, C), :] = turned([hx[k]])
+    def channels(d):
+        return pl.ds(pl.multiple_of(lax.rem(chan + d, nchan) * C, C), C)
+
+    def shift_inputs(d, j):
+        who = channels(d)
+        count = x_starts[j + 1] - x_starts[j]
+        if j == 0:
+            build_shifts(xs, who, hc[who, :], jnp.where(lat == 1, 0, H + 1 - count), count + 1)
+        else:
+            build_shifts(xs, who, hc[who, :], walk(x_starts[j], count) + 1, count)
+
+    for d in range(nchan):
+        back = lax.rem(chan + nchan - d, nchan)
+        for c in halo_copies[d * 5 : d * 5 + 5]:
+            c.wait()
+        hc[pl.ds(pl.multiple_of(back * C, C), C), :] = turned([hx[back]])
+        if d == 0:
+            for j in range(PIECES):
+                shift_inputs(0, j)
 
     ring = nlon * nlat
     spot = lon * nlat + lat
@@ -156,7 +171,7 @@
     base = pl.multiple_of(lat * half, half)
     far = pl.ds(pl.multiple_of(other * half, half), half)
     core_copies, bias_copies, dx_copies = [], [], []
-    dx_starts = [0] + [step * j - 1 for j in range(1, PIECES)] + [H]
+    dx_starts = [0] + [k - 1 for k in g_starts[1:-1]] + [H]
     if R > group_rows:
         for g in range(3):
             dwp[g, pl.ds(group_rows, R - group_rows), :] = jnp.zeros((R - group_rows, CA), F32)
@@ -164,15 +179,16 @@
 
     def input_grad(j):
         grad_copies, row = pending[j]
+        step = g_starts[j + 1] - g_starts[j]
         for c in grad_copies:
             c.wait()
         if j == 0:
             sides = turned([hg[j, 0], hgo[0], hg[j, 1], hgo[1]])
-            build_shifts(gs, sides, jnp.where(lat == 1, 0, H + 1 - step), step + 1)
+            build_shifts(gs, slice(None), sides, jnp.where(lat == 1, 0, H + 1 - step), step + 1)
         else:
             blank = jnp.zeros((H, C), BF)
             sides = turned([hg[j, 0], blank, hg[j, 1], blank])
-            build_shifts(gs, sides, row + 1, step)
+            build_shifts(gs, slice(None), sides, row + 1, step)
         count = dx_starts[j + 1] - dx_starts[j]
         row = walk(dx_starts[j], count)
         stack = jnp.concatenate(
@@ -195,12 +211,10 @@
         final = j == PIECES - 1
         for c in x_copies[j]:
             c.wait()
-        count = x_starts[j + 1] - x_starts[j]
-        if j == 0:
-            build_shifts(xs, hc[...], jnp.where(lat == 1, 0, H + 1 - count), count + 1)
-        else:
-            build_shifts(xs, hc[...], walk(x_starts[j], count) + 1, count)
-        row = walk(j * step, step)
+        for d in range(1, nchan):
+            shift_inputs(d, j)
+        step = g_starts[j + 1] - g_starts[j]
+        row = walk(g_starts[j], step)
         stack = jnp.concatenate(
             [xs[q, :, cols(row + p, step)] for p in range(3) for q in range(3)], axis=0
         )

time: 45.6 us -> 46.3 us (1.015)
  Pallas kernels: 40.7 us -> 41.4 us
    pallas_call x1, Pallas kernels: 40.7 us -> 41.4 us  [local(): pl.pallas_call(functools.partial(kernel, sizes), out_shape=(jax.ShapeDtyp...]
where the time goes in v7:
time: 46.3 us; the launch traced here: 46.1 us
  Pallas kernels  41.4 us (89%)
  local copies, waits for them, and re-layouts  2.92 us (6%)
  other arithmetic  1.13 us (2%)
  between operations  0.67 us (1%)
    pallas_call x1, Pallas kernels, local(): pl.pallas_call(functools.partial(kernel, sizes), out_shape=(jax.ShapeDtyp...  41.4 us
    reshape x1, local copies, waits for them, and re-layouts, local(): cotangent.reshape(C, L)  1.5 us
    unnamed x6, local copies, waits for them, and re-layouts  1.42 us
    reshape x1, other arithmetic, local(): weight_grad = dw[:, :3 * C].astype(F32).reshape(3, 3, C, CA)  1.13 us

profile of v7, /device:TPU:0, one launch (start us, length us, event | category | flops | bytes accessed | tf_op | source)
XLA Modules:
  0.0 46.1 jit_solution(14291546879951112042)
XLA Ops:
  0.6 0.0 copy-start.1
  0.6 0.0 copy-start
  0.7 1.5 %copy_bitcast_fusion = (bf16[128,2048]{1,0:T(8,128)(2,1)S(1)}, bf16[128,2048]{1,0:T(8,128)(2,1)S(1)}) fusion(bf16[16,8,16,128]{3,2,1,0:T(8,128)(2,1)} %bitcast.19, bf16[16,8,16,128]{3,2,1,0:T(8,128)(2,1)} %bitcast.20), kind=kLoop, calls=%fused_computation | loop fusion | bytes 2097152 | tf_op jit(solution)/shard_map/reshape | solution.py:384
  2.2 0.0 copy-done.1
  2.2 0.0 copy-done
  2.2 41.4 %conv_backward.1 = (bf16[128,2048]{1,0:T(8,128)(2,1)S(1)}, bf16[3,384,256]{2,1,0:T(8,128)(2,1)S(1)}, f32[1,128]{1,0:T(1,128)S(1)}) custom-call(bf16[128,2048]{1,0:T(8,128)(2,1)S(1)} %get-tuple-element.10.x_ref, bf16[128,2048]{1,0:T(8,128)(2,1)S(1)} %get-tuple-element.9.ct_ref, bf16[1152,256]{1,0:T(8,128)(2,1)S(1)} %bitcast.15, f32[1,128]{1,0:T(1,128)S(1)} %bitcast.16), custom_call_target="tpu_custom_call" | custom-call | flops 3623878656 | bytes 2097152 | tf_op jit(solution)/shard_map/conv_backward/pallas_call | solution.py:332
  43.6 0.9 %copy.9 = bf16[16,8,16,128]{3,2,1,0:T(8,128)(2,1)} copy(bf16[16,8,16,128]{3,1,2,0:T(8,128)(2,1)S(1)} %bitcast.14) | data formatting | bytes 1048576
  44.5 1.1 %convert.1 = f32[3,3,128,256]{3,2,1,0:T(8,128)} convert(bf16[3,3,128,256]{3,2,1,0:T(8,128)(2,1)S(1)} %bitcast.13) | non-fusion elementwise | flops 294912 | bytes 1769472 | tf_op jit(solution)/shard_map/reshape | solution.py:388
  45.6 0.5 %copy.13 = f32[128]{0:T(128)} copy(f32[128]{0:T(128)S(1)} %bitcast.17) | data formatting | bytes 1024
Async XLA Ops:
  0.6 1.5 %copy-start.1 = (f32[128]{0:T(128)S(1)}, f32[128]{0:T(128)}, u32[]{:S(2)}) copy-start(f32[128]{0:T(128)} %param.7) | copy-start | bytes 1540
  0.6 1.5 %copy-start = (bf16[3,3,128,256]{3,2,1,0:T(8,128)(2,1)S(1)}, bf16[3,3,128,256]{3,2,1,0:T(8,128)(2,1)}, u32[]{:S(2)}) copy-start(bf16[3,3,128,256]{3,2,1,0:T(8,128)(2,1)} %param.6) | copy-start | bytes 1769476

commit v8 on v5

--- a/solution.py
+++ b/solution.py
@@ -123,7 +123,6 @@
 
     for t in range(9):
         w2[:, pl.ds(t * CA, CA)] = w_ref[pl.ds(t * C, C), :]
-    wt[...] = jnp.transpose(w_ref[...])
     bias_col = jnp.transpose(jnp.broadcast_to(b_ref[...], (128, C)))[:, :1]
 
     def build_shifts(field, columns, start, count):
@@ -160,19 +159,14 @@
     if R > group_rows:
         for g in range(3):
             dwp[g, pl.ds(group_rows, R - group_rows), :] = jnp.zeros((R - group_rows, CA), F32)
-    pending = []
+    grad_copies = []
 
     def input_grad(j):
-        grad_copies, row = pending[j]
-        for c in grad_copies:
-            c.wait()
         if j == 0:
-            sides = turned([hg[j, 0], hgo[0], hg[j, 1], hgo[1]])
-            build_shifts(gs, sides, jnp.where(lat == 1, 0, H + 1 - step), step + 1)
-        else:
-            blank = jnp.zeros((H, C), BF)
-            sides = turned([hg[j, 0], blank, hg[j, 1], blank])
-            build_shifts(gs, sides, row + 1, step)
+            for c in grad_copies:
+                c.wait()
+            sides = turned([hg[0], hgo[0], hg[1], hgo[1]])
+            build_shifts(gs, sides, other, H + 1)
         count = dx_starts[j + 1] - dx_starts[j]
         row = walk(dx_starts[j], count)
         stack = jnp.concatenate(
@@ -208,20 +202,18 @@
         upstream = ct_ref[:, cols(row, step)].astype(F32)
         grad = (upstream * gelu_slope(preact)).astype(BF)
         gs[1, :, cols(row + 1, step)] = grad
-        gedge[j] = edges(grad, row)
-        grad_copies = []
-        if j == 0:
+        if final:
+            gedge[...] = edges(gs[1, :, pl.ds(W, L)], 0)
             grad_copies.append(
                 copy(gs.at[1, :, cols(other * (H - 1) + 1, 1)], gs.at[1, :, to_row], grow_sem, (0,), at(lon, chan, other))
             )
-        for side in range(2):
-            lon_to = lax.rem(lon + (nlon - 1 if side == 0 else 1), nlon)
-            tile = gedge.at[j, pl.ds(side * H, H)]
-            grad_copies.append(copy(tile, hg.at[j, 1 - side], gcol_sem, (j, side), at(lon_to, chan, lat)))
-            if j == 0:
+            for side in range(2):
+                lon_to = lax.rem(lon + (nlon - 1 if side == 0 else 1), nlon)
+                tile = gedge.at[pl.ds(side * H, H)]
+                grad_copies.append(copy(tile, hg.at[1 - side], gcol_sem, (side,), at(lon_to, chan, lat)))
                 grad_copies.append(copy(tile, hgo.at[1 - side], gother_sem, (side,), at(lon_to, chan, other)))
-        for c in grad_copies:
-            c.start()
+            for c in grad_copies:
+                c.start()
         for p in range(3):
             for q in range(3):
                 here = pl.ds(q * C, C)
@@ -232,9 +224,8 @@
                 c = copy(dwsend.at[p], dwcore.at[p], core_sem, (p,), at(lon, chan, other))
                 c.start()
                 core_copies.append(c)
-        pending.append((grad_copies, row))
-
-    input_grad(0)
+
+    wt[...] = jnp.transpose(w_ref[...])
     rs_copies = []
     for g in range(3):
         core_copies[g].wait()
@@ -250,7 +241,7 @@
             )
             c.start()
             rs_copies[g].append(c)
-    for j in range(1, PIECES):
+    for j in range(PIECES):
         input_grad(j)
     bias[spot] = nt(jnp.ones((8, L), BF), gs[1, :, pl.ds(W, L)])
     for d in range(1, ring):
@@ -332,9 +323,9 @@
             pltpu.VMEM((C, 9 * CA), BF),
             pltpu.VMEM((CA, 9 * C), BF),
             pltpu.VMEM((3, C, wide), BF),
-            pltpu.VMEM((PIECES, 2, H, C), BF),
             pltpu.VMEM((2, H, C), BF),
-            pltpu.VMEM((PIECES, 2 * H, C), BF),
+            pltpu.VMEM((2, H, C), BF),
+            pltpu.VMEM((2 * H, C), BF),
             pltpu.VMEM((3, R, CA), F32),
             pltpu.VMEM((3, half, CA), BF),
             pltpu.VMEM((3, half, CA), BF),
@@ -349,7 +340,7 @@
             dma((2, nchan)),
             dma((2, nchan, 2, 2)),
             dma((2, 1)),
-            dma((2, PIECES, 2)),
+            dma((2, 2)),
             dma((2, 2)),
             dma((2, 3)),
             dma((2, 3, nlon)),

time: 45.6 us -> 45.3 us (level)
  no operation moved by 1% of the time
where the time goes in v8:
time: 45.3 us; the launch traced here: 45.2 us
  Pallas kernels  40.4 us (89%)
  local copies, waits for them, and re-layouts  2.92 us (6%)
  other arithmetic  1.13 us (2%)
  between operations  0.67 us (1%)
    pallas_call x1, Pallas kernels, local(): pl.pallas_call(functools.partial(kernel, sizes), out_shape=(jax.ShapeDtyp...  40.4 us
    reshape x1, local copies, waits for them, and re-layouts, local(): cotangent.reshape(C, L)  1.5 us
    unnamed x6, local copies, waits for them, and re-layouts  1.42 us
    reshape x1, other arithmetic, local(): weight_grad = dw[:, :3 * C].astype(F32).reshape(3, 3, C, CA)  1.13 us

profile of v8, /device:TPU:0, one launch (start us, length us, event | category | flops | bytes accessed | tf_op | source)
XLA Modules:
  0.0 45.2 jit_solution(15699813097990493328)
XLA Ops:
  0.6 0.0 copy-start.1
  0.6 0.0 copy-start
  0.7 1.5 %copy_bitcast_fusion = (bf16[128,2048]{1,0:T(8,128)(2,1)S(1)}, bf16[128,2048]{1,0:T(8,128)(2,1)S(1)}) fusion(bf16[16,8,16,128]{3,2,1,0:T(8,128)(2,1)} %bitcast.19, bf16[16,8,16,128]{3,2,1,0:T(8,128)(2,1)} %bitcast.20), kind=kLoop, calls=%fused_computation | loop fusion | bytes 2097152 | tf_op jit(solution)/shard_map/reshape | solution.py:361
  2.2 0.0 copy-done.1
  2.2 0.0 copy-done
  2.2 40.4 %conv_backward.1 = (bf16[128,2048]{1,0:T(8,128)(2,1)S(1)}, bf16[3,384,256]{2,1,0:T(8,128)(2,1)S(1)}, f32[1,128]{1,0:T(1,128)S(1)}) custom-call(bf16[128,2048]{1,0:T(8,128)(2,1)S(1)} %get-tuple-element.10.x_ref, bf16[128,2048]{1,0:T(8,128)(2,1)S(1)} %get-tuple-element.9.ct_ref, bf16[1152,256]{1,0:T(8,128)(2,1)S(1)} %bitcast.15, f32[1,128]{1,0:T(1,128)S(1)} %bitcast.16), custom_call_target="tpu_custom_call" | custom-call | flops 3623878656 | bytes 2097152 | tf_op jit(solution)/shard_map/conv_backward/pallas_call | solution.py:309
  42.6 0.9 %copy.9 = bf16[16,8,16,128]{3,2,1,0:T(8,128)(2,1)} copy(bf16[16,8,16,128]{3,1,2,0:T(8,128)(2,1)S(1)} %bitcast.14) | data formatting | bytes 1048576
  43.5 1.1 %convert.1 = f32[3,3,128,256]{3,2,1,0:T(8,128)} convert(bf16[3,3,128,256]{3,2,1,0:T(8,128)(2,1)S(1)} %bitcast.13) | non-fusion elementwise | flops 294912 | bytes 1769472 | tf_op jit(solution)/shard_map/reshape | solution.py:365
  44.7 0.5 %copy.13 = f32[128]{0:T(128)} copy(f32[128]{0:T(128)S(1)} %bitcast.17) | data formatting | bytes 1024
Async XLA Ops:
  0.6 1.5 %copy-start.1 = (f32[128]{0:T(128)S(1)}, f32[128]{0:T(128)}, u32[]{:S(2)}) copy-start(f32[128]{0:T(128)} %param.7) | copy-start | bytes 1540
  0.6 1.5 %copy-start = (bf16[3,3,128,256]{3,2,1,0:T(8,128)(2,1)S(1)}, bf16[3,3,128,256]{3,2,1,0:T(8,128)(2,1)}, u32[]{:S(2)}) copy-start(bf16[3,3,128,256]{3,2,1,0:T(8,128)(2,1)} %param.6) | copy-start | bytes 1769476

commit v9 on v8

--- a/solution.py
+++ b/solution.py
@@ -123,6 +123,7 @@
 
     for t in range(9):
         w2[:, pl.ds(t * CA, CA)] = w_ref[pl.ds(t * C, C), :]
+    wt[...] = jnp.transpose(w_ref[...])
     bias_col = jnp.transpose(jnp.broadcast_to(b_ref[...], (128, C)))[:, :1]
 
     def build_shifts(field, columns, start, count):
@@ -225,7 +226,7 @@
                 c.start()
                 core_copies.append(c)
 
-    wt[...] = jnp.transpose(w_ref[...])
+    input_grad(0)
     rs_copies = []
     for g in range(3):
         core_copies[g].wait()
@@ -241,7 +242,7 @@
             )
             c.start()
             rs_copies[g].append(c)
-    for j in range(PIECES):
+    for j in range(1, PIECES):
         input_grad(j)
     bias[spot] = nt(jnp.ones((8, L), BF), gs[1, :, pl.ds(W, L)])
     for d in range(1, ring):

time: 45.3 us -> 48.5 us (1.071)
  Pallas kernels: 40.4 us -> 43.6 us
    pallas_call x1, Pallas kernels: 40.4 us -> 43.6 us  [local(): pl.pallas_call(functools.partial(kernel, sizes), out_shape=(jax.ShapeDtyp...]
where the time goes in v9:
time: 48.5 us; the launch traced here: 48.3 us
  Pallas kernels  43.6 us (90%)
  local copies, waits for them, and re-layouts  2.92 us (6%)
  other arithmetic  1.13 us (2%)
  between operations  0.67 us (1%)
    pallas_call x1, Pallas kernels, local(): pl.pallas_call(functools.partial(kernel, sizes), out_shape=(jax.ShapeDtyp...  43.6 us
    reshape x1, local copies, waits for them, and re-layouts, local(): cotangent.reshape(C, L)  1.5 us
    unnamed x6, local copies, waits for them, and re-layouts  1.42 us
    reshape x1, other arithmetic, local(): weight_grad = dw[:, :3 * C].astype(F32).reshape(3, 3, C, CA)  1.13 us

profile of v9, /device:TPU:0, one launch (start us, length us, event | category | flops | bytes accessed | tf_op | source)
XLA Modules:
  0.0 48.3 jit_solution(3487754843053560888)
XLA Ops:
  0.6 0.0 copy-start.1
  0.6 0.0 copy-start
  0.7 1.5 %copy_bitcast_fusion = (bf16[128,2048]{1,0:T(8,128)(2,1)S(1)}, bf16[128,2048]{1,0:T(8,128)(2,1)S(1)}) fusion(bf16[16,8,16,128]{3,2,1,0:T(8,128)(2,1)} %bitcast.19, bf16[16,8,16,128]{3,2,1,0:T(8,128)(2,1)} %bitcast.20), kind=kLoop, calls=%fused_computation | loop fusion | bytes 2097152 | tf_op jit(solution)/shard_map/reshape | solution.py:362
  2.2 0.0 copy-done.1
  2.2 0.0 copy-done
  2.2 43.6 %conv_backward.1 = (bf16[128,2048]{1,0:T(8,128)(2,1)S(1)}, bf16[3,384,256]{2,1,0:T(8,128)(2,1)S(1)}, f32[1,128]{1,0:T(1,128)S(1)}) custom-call(bf16[128,2048]{1,0:T(8,128)(2,1)S(1)} %get-tuple-element.10.x_ref, bf16[128,2048]{1,0:T(8,128)(2,1)S(1)} %get-tuple-element.9.ct_ref, bf16[1152,256]{1,0:T(8,128)(2,1)S(1)} %bitcast.15, f32[1,128]{1,0:T(1,128)S(1)} %bitcast.16), custom_call_target="tpu_custom_call" | custom-call | flops 3623878656 | bytes 2097152 | tf_op jit(solution)/shard_map/conv_backward/pallas_call | solution.py:310
  45.8 0.9 %copy.9 = bf16[16,8,16,128]{3,2,1,0:T(8,128)(2,1)} copy(bf16[16,8,16,128]{3,1,2,0:T(8,128)(2,1)S(1)} %bitcast.14) | data formatting | bytes 1048576
  46.7 1.1 %convert.1 = f32[3,3,128,256]{3,2,1,0:T(8,128)} convert(bf16[3,3,128,256]{3,2,1,0:T(8,128)(2,1)S(1)} %bitcast.13) | non-fusion elementwise | flops 294912 | bytes 1769472 | tf_op jit(solution)/shard_map/reshape | solution.py:366
  47.8 0.5 %copy.13 = f32[128]{0:T(128)} copy(f32[128]{0:T(128)S(1)} %bitcast.17) | data formatting | bytes 1024
Async XLA Ops:
  0.6 1.5 %copy-start.1 = (f32[128]{0:T(128)S(1)}, f32[128]{0:T(128)}, u32[]{:S(2)}) copy-start(f32[128]{0:T(128)} %param.7) | copy-start | bytes 1540
  0.6 1.5 %copy-start = (bf16[3,3,128,256]{3,2,1,0:T(8,128)(2,1)S(1)}, bf16[3,3,128,256]{3,2,1,0:T(8,128)(2,1)}, u32[]{:S(2)}) copy-start(bf16[3,3,128,256]{3,2,1,0:T(8,128)(2,1)} %param.6) | copy-start | bytes 1769476
